TPU v7x, 128 devices: a whole 4x4x4 slice. The times are simulated.
128 devices in a mesh: dp: 16 (over z, y_hi, core), frame: 8 (over x, y_lo).
Axes of the slice: x: 4, y: 4 (y_hi: 2, y_lo: 2; y = y_hi * 2 + y_lo), z: 4, core: 2. Of those that a mesh axis runs over, the one named last changes fastest.
Arguments:
- clips: bfloat16 [16, 16, 64, 1152], P('dp', 'frame'), may hold values from -6 to 6
- params: bfloat16 [1152, 4608], replicated, may hold values from -0.1875 to 0.1875
- direction: bfloat16 [1152, 4608], replicated, may hold values from -0.1875 to 0.1875
Outputs:
- tangent_out: bfloat16 [16, 16, 64, 1152], P('dp', 'frame')
- gnv: float32 [1152, 4608], P(('dp', 'frame'))
All inputs are finite; a program needn't handle non-finite values.
Results may differ from a plain program's by a relative error of at most 0.025.
Values may be sent and summed in bfloat16 or wider, within the bound.
A program may use at most 192 MiB of HBM per device.

v0:
```python
import jax
import jax.numpy as jnp
from jax import lax
from jax.experimental import pallas as pl
from jax.experimental.pallas import tpu as pltpu
from jax.sharding import PartitionSpec as P

MESH = pl.DeviceIdType.MESH
F32 = jnp.float32
BF16 = jnp.bfloat16

D = 1152
HD = 72
HEADS = 8
QKV = 1792
OUT = 640
SCALE = HD ** (-0.5)

S_QKV, S_OUT, T_QKV, T_OUT = 0, 1664, 2304, 3968

HEAD_WINDOWS = [
    (h * HD, (h + 1) * HD, h * HD // 128 * 128, -(-(h + 1) * HD // 128) * 128)
    for h in range(HEADS)
]

LEFTS = ["gy_z", "h2_z", "h2_y", "h2_x", "g_x", "h1_z", "h1_y", "h1_x"]
RIGHTS = {"q1": QKV, "o1": OUT, "q2": QKV, "o2": OUT}

JOBS = [
    (14 * 128, 1024, "zxy", [(0, 512, [("gy_z", "o1", 128)]), (512, 1024, [("h2_z", "q2", 0)])]),
    (22 * 128, 896, "yzx", [(0, 896, [("h2_y", "q2", 512)])]),
    (
        29 * 128,
        896,
        "xyz",
        [
            (0, 256, [("h2_x", "q2", 1408)]),
            (256, 384, [("h2_x", "q2", 1664), ("g_x", "o2", 0)]),
            (384, 896, [("g_x", "o2", 128)]),
        ],
    ),
    (
        10 * 128,
        512,
        "zxy",
        [(0, 384, [("h1_z", "q1", 1280)]), (384, 512, [("h1_z", "q1", 1664), ("gy_z", "o1", 0)])],
    ),
    (5 * 128, 640, "yzx", [(0, 640, [("h1_y", "q1", 640)])]),
    (0, 640, "xyz", [(0, 640, [("h1_x", "q1", 0)])]),
]
N_JOBS = len(JOBS)


def row_moves(order):
    moves = []
    for z in range(4):
        for yh in range(2):
            for c in range(2):
                base = 288 * z + 144 * yh + 72 * c
                if order == "z":
                    moves.append((base, c, 144 * z + 72 * yh, 72))
                    continue
                for x in range(4):
                    if order == "x":
                        moves.append((base + 18 * x, c, 144 * x + 36 * z + 18 * yh, 18))
                        continue
                    for yl in range(2):
                        moves.append((base + 18 * x + 9 * yl, c, 144 * (2 * yh + yl) + 36 * z + 9 * x, 9))
    return moves


def second_rows(axes, second, third):
    if axes == "zxy":
        return 72 * (third // 2) + 18 * second + 9 * (third % 2)
    if axes == "yzx":
        return 36 * second + 9 * third
    return 36 * third + 9 * second


def nn(a, b):
    return jnp.dot(a, b, preferred_element_type=F32)


def nt(a, b):
    return lax.dot_general(a, b, (((1,), (1,)), ((), ())), preferred_element_type=F32)


def tn(a, b):
    return lax.dot_general(a, b, (((0,), (0,)), ((), ())), preferred_element_type=F32)


def left_64(x):
    return pltpu.roll(x, x.shape[1] - 64, 1)


def right_64(x):
    return pltpu.roll(x, 64, 1)


def lane_mask(lo, hi, a, b):
    lane = lax.broadcasted_iota(jnp.int32, (1, b - a), 1) + a
    return (lane >= lo) & (lane < hi)


def add_head(tiles, head, value):
    lo, hi, a, b = HEAD_WINDOWS[head]
    for j in range(a // 128, b // 128):
        piece = value[:, j * 128 - a : (j + 1) * 128 - a]
        mask = lane_mask(lo, hi, j * 128, (j + 1) * 128)
        old = jnp.zeros_like(piece) if tiles[j] is None else tiles[j]
        tiles[j] = jnp.where(mask, piece, old)


def attend(qkv, dqkv, kx, dkx, pn_ref, mask):
    out, tan = [None] * 5, [None] * 5
    for h in range(HEADS):
        lo, hi, a, b = HEAD_WINDOWS[h]
        lanes = jnp.where(lane_mask(lo, hi, a, b), 1.0, 0.0).astype(BF16)
        q = qkv[:, a:b] * lanes
        dq = dqkv[:, a:b] * lanes
        k, dk = kx[:, a:b], dkx[:, a:b]
        v, dv = qkv[:, 1152 + a : 1152 + b], dqkv[:, 1152 + a : 1152 + b]
        e = jnp.where(mask, jnp.exp(nt(q, k) * SCALE), 0.0)
        pn = e * (1.0 / jnp.sum(e, axis=1, keepdims=True))
        pn_ref[h] = pn
        p = pn.astype(BF16)
        ds = (nt(dq, k) + nt(q, dk)) * SCALE
        dp = (pn * (ds - jnp.sum(pn * ds, axis=1, keepdims=True))).astype(BF16)
        add_head(out, h, nn(p, v))
        add_head(tan, h, nn(dp, v) + nn(p, dv))
    return jnp.concatenate(out, axis=1), jnp.concatenate(tan, axis=1)


def attend_back(qkv, kx, pn_ref, go, grad_ref):
    gq, gk, gv = [None] * 5, [None] * 5, [None] * 5
    for h in range(HEADS):
        lo, hi, a, b = HEAD_WINDOWS[h]
        lanes = jnp.where(lane_mask(lo, hi, a, b), 1.0, 0.0).astype(BF16)
        gow = go[:, a:b]
        gp = nt(gow * lanes, qkv[:, 1152 + a : 1152 + b]).astype(BF16).astype(F32)
        pn = pn_ref[h]
        gs = (pn * (gp - jnp.sum(gp * pn, axis=1, keepdims=True)) * SCALE).astype(BF16)
        add_head(gq, h, nn(gs, kx[:, a:b]))
        add_head(gk, h, tn(gs, qkv[:, a:b]))
        add_head(gv, h, tn(pn.astype(BF16), gow))
    gkr = right_64(jnp.concatenate(gk, axis=1))
    for j in range(4):
        grad_ref[:, j * 128 : (j + 1) * 128] = gq[j].astype(BF16)
    grad_ref[:, 512:640] = (gq[4] + gkr[:, :128]).astype(BF16)
    grad_ref[:, 640:1152] = gkr[:, 128:].astype(BF16)
    for j in range(5):
        grad_ref[:, 1152 + j * 128 : 1280 + j * 128] = gv[j].astype(BF16)


def norm_parts(x):
    centred = x - jnp.mean(x, axis=-1, keepdims=True)
    rstd = lax.rsqrt(jnp.mean(centred * centred, axis=-1, keepdims=True) + 1e-06)
    return centred * rstd, rstd


def norm_tangent(normed, rstd, dx):
    return rstd * (
        dx
        - jnp.mean(dx, axis=-1, keepdims=True)
        - normed * jnp.mean(normed * dx, axis=-1, keepdims=True)
    )


def shape_list():
    v = pltpu.VMEM
    dma = pltpu.SemaphoreType.DMA
    scratch = {
        "wp": v((D, 4608), BF16),
        "wd": v((D, 4608), BF16),
        "h1": v((128, D), BF16),
        "qkv1": v((128, QKV), BF16),
        "dqkv1": v((128, QKV), BF16),
        "kx1": v((128, OUT), BF16),
        "dkx": v((128, OUT), BF16),
        "pn1": v((HEADS, 128, 128), F32),
        "qkv2": v((128, QKV), BF16),
        "dqkv2": v((128, QKV), BF16),
        "kx2": v((128, OUT), BF16),
        "pn2": v((HEADS, 128, 128), F32),
        "go": v((128, OUT), BF16),
        "clips_s": v((8, 16, D), BF16),
        "clips_r": v((8, 16, D), BF16),
        "attn_s": v((8, 16, 2 * OUT), BF16),
        "attn_r": v((8, 16, 2 * OUT), BF16),
        "go_s": v((8, 16, OUT), BF16),
        "go_r": v((8, 16, OUT), BF16),
        "tan_s": v((8, 16, D), BF16),
        "tan_r": v((8, 16, D), BF16),
        "lt": v((D, 128), F32),
        "lts": v((2, 576, 128), F32),
        "left": v((len(LEFTS), 576, 256), BF16),
        "left_s": v((len(LEFTS), 576, 128), BF16),
    }
    for name, width in RIGHTS.items():
        scratch["r_" + name] = v((256, width), BF16)
    for i, (_, n, _, _) in enumerate(JOBS):
        scratch[f"p{i}"] = v((4, 144, n), BF16)
        scratch[f"v{i}"] = v((3, 144, n), BF16)
        scratch[f"s2_{i}"] = v((4, 48, n), BF16)
        scratch[f"v2_{i}"] = v((3, 48, n), BF16)
        scratch[f"s3_{i}"] = v((4, 16, n), BF16)
        scratch[f"v3_{i}"] = v((3, 16, n), BF16)
    scratch["acc1"] = v((144, 1024), F32)
    scratch["acc2"] = v((48, 1024), F32)
    scratch["pad2"] = v((48, 1024), F32)
    scratch["pad3"] = v((16, 1024), F32)
    scratch["w_sem"] = dma((8,))
    scratch["a_send"] = dma((4, 7))
    scratch["a_recv"] = dma((4, 7))
    scratch["c_send"] = dma((len(LEFTS) + len(RIGHTS),))
    scratch["c_recv"] = dma((len(LEFTS) + len(RIGHTS),))
    scratch["rs_send"] = dma((N_JOBS, 3, 3))
    scratch["rs_recv"] = dma((N_JOBS, 3, 3))
    return scratch


SCRATCH = shape_list()


def kernel(clips_ref, params_ref, direction_ref, tan_ref, gnv_ref, *scratch_refs):
    s = dict(zip(SCRATCH, scratch_refs))
    dp, fr = lax.axis_index("dp"), lax.axis_index("frame")
    core, y_hi, z = dp % 2, dp // 2 % 2, dp // 4
    x, y_lo = fr // 2, fr % 2
    where = {"z": z, "y": 2 * y_hi + y_lo, "x": x}

    def device(at, c):
        return (at["z"] * 4 + at["y"] // 2 * 2 + c, at["x"] * 2 + at["y"] % 2)

    def along(axis, k):
        at = dict(where)
        at[axis] = (at[axis] + k) % 4
        return device(at, core)

    partner = (dp + 1 - 2 * core, fr)

    def remote(src, dst, send, recv, to):
        copy = pltpu.make_async_remote_copy(
            src_ref=src, dst_ref=dst, send_sem=send, recv_sem=recv, device_id=to, device_id_type=MESH
        )
        copy.start()
        sent.append(copy)
        return copy

    sent = []

    loads = []
    for i, (lo, hi) in enumerate([(0, 1792), (1792, 2304), (2304, 4096), (4096, 4608)]):
        pair = []
        for j, (src, dst) in enumerate([(params_ref, s["wp"]), (direction_ref, s["wd"])]):
            copy = pltpu.make_async_copy(src.at[:, lo:hi], dst.at[:, lo:hi], s["w_sem"].at[2 * i + j])
            copy.start()
            pair.append(copy)
        loads.append(pair)

    def loaded(i):
        for copy in loads[i]:
            copy.wait()

    barrier = pltpu.get_barrier_semaphore()
    peers = [along(axis, k) for axis in "zyx" for k in (1, 2, 3)]
    peers += [(dp, (x + k) % 4 * 2 + 1 - y_lo) for k in (1, 2, 3)]
    peers.append(partner)
    for peer in peers:
        pl.semaphore_signal(barrier, inc=1, device_id=peer, device_id_type=MESH)

    natural = clips_ref[...].astype(F32)
    tokens = jnp.concatenate(
        [natural[f, 8 * t : 8 * t + 8] for t in range(8) for f in range(2)], axis=0
    )
    s["clips_s"][...] = tokens.astype(BF16).reshape(8, 16, D)
    h1f, _ = norm_parts(tokens)
    s["h1"][...] = h1f.astype(BF16)

    pl.semaphore_wait(barrier, len(peers))

    def frame_exchange(which, src, dst):
        copies = []
        for k in range(1, 8):
            t = (fr + k) % 8
            copies.append(
                remote(src.at[t], dst.at[fr], s["a_send"].at[which, k - 1], s["a_recv"].at[which, k - 1], (dp, t))
            )
        dst[fr] = src[fr]
        return copies

    def arrived(copies):
        for copy in copies:
            copy.wait_recv()

    clips_copies = frame_exchange(0, s["clips_s"], s["clips_r"])

    left_copies = {}

    def prepare_left(value, names):
        s["lt"][...] = value.T
        for name in names:
            i = LEFTS.index(name)
            for src, c, dst, rows in row_moves(name[-1]):
                s["lts"][c, dst : dst + rows, :] = s["lt"][src : src + rows, :]
            s["left"][i, :, 0:128] = s["lts"][core].astype(BF16)
            s["left_s"][i] = s["lts"][1 - core].astype(BF16)
            left_copies[name] = remote(
                s["left_s"].at[i], s["left"].at[i, :, pl.ds(128, 128)], s["c_send"].at[i], s["c_recv"].at[i], partner
            )

    right_copies = {}

    def share_right(name):
        i = len(LEFTS) + list(RIGHTS).index(name)
        ref = s["r_" + name]
        right_copies[name] = remote(
            ref.at[pl.ds(0, 128)], ref.at[pl.ds(128, 128)], s["c_send"].at[i], s["c_recv"].at[i], partner
        )

    loaded(0)
    for lo in range(0, QKV, 256):
        s["qkv1"][:, lo : lo + 256] = nn(s["h1"][...], s["wp"][:, lo : lo + 256]).astype(BF16)
        s["dqkv1"][:, lo : lo + 256] = nn(s["h1"][...], s["wd"][:, lo : lo + 256]).astype(BF16)

    def align_keys(qkv, kx):
        kx[...] = left_64(qkv[:, 512:1152].astype(F32)).astype(BF16)

    row = lax.broadcasted_iota(jnp.int32, (128, 128), 0)
    col = lax.broadcasted_iota(jnp.int32, (128, 128), 1)
    same_frame = row // 8 % 2 == col // 8 % 2
    same_patch = row % 8 == col % 8
    align_keys(s["qkv1"], s["kx1"])
    align_keys(s["dqkv1"], s["dkx"])
    o1, do1 = attend(s["qkv1"], s["dqkv1"], s["kx1"], s["dkx"], s["pn1"], same_frame)
    s["attn_s"][:, :, 0:OUT] = right_64(o1).astype(BF16).reshape(8, 16, OUT)
    s["attn_s"][:, :, OUT:] = right_64(do1).astype(BF16).reshape(8, 16, OUT)
    attn_copies = frame_exchange(1, s["attn_s"], s["attn_r"])

    prepare_left(h1f.astype(BF16).astype(F32), ["h1_z", "h1_y", "h1_x"])

    arrived(clips_copies)
    loaded(1)
    arrived(attn_copies)
    clips_p = s["clips_r"][...].reshape(128, D).astype(F32)
    o1x = s["attn_r"][:, :, 0:OUT].reshape(128, OUT)
    do1x = s["attn_r"][:, :, OUT:].reshape(128, OUT)
    s["r_o1"][0:128, :] = o1x
    share_right("o1")
    s_out, v_sout = s["wp"][:, S_OUT : S_OUT + OUT], s["wd"][:, S_OUT : S_OUT + OUT]
    y = (clips_p + nt(o1x, s_out)).astype(BF16).astype(F32)
    dy = (nt(do1x, s_out) + nt(o1x, v_sout)).astype(BF16).astype(F32)
    h2f, rstd = norm_parts(y)
    h2 = h2f.astype(BF16)
    dh2 = norm_tangent(h2f, rstd, dy).astype(BF16)
    loaded(2)
    for lo in range(0, QKV, 256):
        wp = s["wp"][:, T_QKV + lo : T_QKV + lo + 256]
        wd = s["wd"][:, T_QKV + lo : T_QKV + lo + 256]
        s["qkv2"][:, lo : lo + 256] = nn(h2, wp).astype(BF16)
        s["dqkv2"][:, lo : lo + 256] = (nn(dh2, wp) + nn(h2, wd)).astype(BF16)
    align_keys(s["qkv2"], s["kx2"])
    align_keys(s["dqkv2"], s["dkx"])
    o2, do2 = attend(s["qkv2"], s["dqkv2"], s["kx2"], s["dkx"], s["pn2"], same_patch)
    o2x, do2x = right_64(o2).astype(BF16), right_64(do2).astype(BF16)
    s["r_o2"][0:128, :] = o2x
    share_right("o2")
    loaded(3)
    t_out, v_tout = s["wp"][:, T_OUT : T_OUT + OUT], s["wd"][:, T_OUT : T_OUT + OUT]
    tangent = (dy + nt(do2x, t_out) + nt(o2x, v_tout)).astype(BF16)
    s["tan_s"][...] = tangent.reshape(8, 16, D)
    tan_copies = frame_exchange(3, s["tan_s"], s["tan_r"])
    g = (tangent.astype(F32) * (16384 ** (-0.5))).astype(BF16)
    s["go"][...] = left_64(nn(g, t_out)).astype(BF16)
    attend_back(s["qkv2"], s["kx2"], s["pn2"], s["go"], s["r_q2"].at[pl.ds(0, 128)])
    share_right("q2")
    gq2 = s["r_q2"][0:128, :]
    gh2 = nt(gq2, s["wp"][:, T_QKV : T_QKV + QKV])
    gy = (g.astype(F32) + norm_tangent(h2f, rstd, gh2)).astype(BF16)
    s["go_s"][...] = nn(gy, s_out).astype(BF16).reshape(8, 16, OUT)
    go_copies = frame_exchange(2, s["go_s"], s["go_r"])
    prepare_left(gy.astype(F32), ["gy_z"])
    prepare_left(h2.astype(F32), ["h2_z", "h2_y", "h2_x"])
    prepare_left(g.astype(F32), ["g_x"])

    arrived(tan_copies)
    tan = s["tan_r"][...].reshape(128, D).astype(F32)
    for f in range(2):
        tan_ref[f] = jnp.concatenate(
            [tan[16 * t + 8 * f : 16 * t + 8 * f + 8] for t in range(8)], axis=0
        ).astype(BF16)
    arrived(go_copies)
    s["go"][...] = left_64(s["go_r"][...].reshape(128, OUT).astype(F32)).astype(BF16)
    attend_back(s["qkv1"], s["kx1"], s["pn1"], s["go"], s["r_q1"].at[pl.ds(0, 128)])
    share_right("q1")

    for copy in left_copies.values():
        copy.wait_recv()
    for copy in right_copies.values():
        copy.wait_recv()

    def scatter(job, stage, src, dst):
        axis = JOBS[job][2][stage]
        copies = []
        for k in (1, 2, 3):
            t = (where[axis] + k) % 4
            copies.append(
                remote(
                    src.at[t],
                    dst.at[k - 1],
                    s["rs_send"].at[job, stage, k - 1],
                    s["rs_recv"].at[job, stage, k - 1],
                    along(axis, k),
                )
            )
        return copies

    def total(job, stage, src, dst):
        mine = src[where[JOBS[job][2][stage]]].astype(F32)
        return mine + dst[0].astype(F32) + dst[1].astype(F32) + dst[2].astype(F32)

    s["pad2"][...] = jnp.zeros_like(s["pad2"])
    s["pad3"][...] = jnp.zeros_like(s["pad3"])
    flight = []
    for job, (_, n, _, segments) in enumerate(JOBS):
        for lo, hi, terms in segments:
            acc = None
            for left, right, at in terms:
                term = nn(s["left"][LEFTS.index(left)], s["r_" + right][:, at : at + hi - lo])
                acc = term if acc is None else acc + term
            s[f"p{job}"][:, :, lo:hi] = acc.astype(BF16).reshape(4, 144, hi - lo)
        flight.append(scatter(job, 0, s[f"p{job}"], s[f"v{job}"]))

    for job, (_, n, axes, _) in enumerate(JOBS):
        arrived(flight[job])
        s["acc1"][:, :n] = total(job, 0, s[f"p{job}"], s[f"v{job}"])
        for second in range(4):
            for third in range(4):
                at = second_rows(axes, second, third)
                s["pad2"][9 * third : 9 * third + 9, :n] = s["acc1"][at : at + 9, :n]
            s[f"s2_{job}"][second] = s["pad2"][:, :n].astype(BF16)
        flight[job] = scatter(job, 1, s[f"s2_{job}"], s[f"v2_{job}"])

    for job, (_, n, _, _) in enumerate(JOBS):
        arrived(flight[job])
        s["acc2"][:, :n] = total(job, 1, s[f"s2_{job}"], s[f"v2_{job}"])
        for third in range(4):
            s["pad3"][0:9, :n] = s["acc2"][9 * third : 9 * third + 9, :n]
            s[f"s3_{job}"][third] = s["pad3"][:, :n].astype(BF16)
        flight[job] = scatter(job, 2, s[f"s3_{job}"], s[f"v3_{job}"])

    for job, (first, n, _, _) in enumerate(JOBS):
        arrived(flight[job])
        gnv_ref[:, first : first + n] = total(job, 2, s[f"s3_{job}"], s[f"v3_{job}"])[0:9]

    for copy in sent:
        copy.wait_send()


def body(clips, params, direction):
    tangent, gnv = pl.pallas_call(
        kernel,
        out_shape=(
            jax.ShapeDtypeStruct((2, 64, D), BF16),
            jax.ShapeDtypeStruct((9, 4608), F32),
        ),
        in_specs=[
            pl.BlockSpec(memory_space=pltpu.VMEM),
            pl.BlockSpec(memory_space=pl.ANY),
            pl.BlockSpec(memory_space=pl.ANY),
        ],
        out_specs=(pl.BlockSpec(memory_space=pltpu.VMEM), pl.BlockSpec(memory_space=pltpu.VMEM)),
        scratch_shapes=list(SCRATCH.values()),
        compiler_params=pltpu.CompilerParams(
            collective_id=0, has_side_effects=True, vmem_limit_bytes=62 * 2**20
        ),
    )(clips[0], params, direction)
    return tangent[None], gnv


def solution(mesh):
    in_specs = (P("dp", "frame", None, None), P(), P())
    out_specs = (P("dp", "frame", None, None), P(("dp", "frame"), None))
    return jax.shard_map(body, mesh=mesh, in_specs=in_specs, out_specs=out_specs, check_vma=False)
```

profile of v0, /device:TPU:1, one launch (start us, length us, event | category | flops | bytes accessed | tf_op | source)
XLA Modules:
  0.0 78.4 jit_solution(3786427827087075532)
XLA Ops:
  0.6 74.4 %shard_map.50 = (bf16[2,64,1152]{2,1,0:T(8,128)(2,1)}, f32[9,4608]{1,0:T(8,128)}) custom-call(bf16[2,64,1152]{2,1,0:T(8,128)(2,1)} %bitcast.3, bf16[1152,4608]{1,0:T(8,128)(2,1)} %params_ref.1, bf16[1152,4608]{1,0:T(8,128)(2,1)} %direction_ref.1), custom_call_target="tpu_custom_call" | custom-call | tf_op jit(solution)/shard_map/pallas_call | solution.py:461
  75.0 1.7 %copy.7 = bf16[1,2,64,1152]{3,2,1,0:T(8,128)(2,1)} copy(bf16[1,2,64,1152]{3,2,1,0:T(8,128)(2,1)} %bitcast.2) | data formatting | bytes 589824
  76.7 1.7 %copy.8 = f32[9,4608]{1,0:T(8,128)} copy(f32[9,4608]{1,0:T(8,128)} %get-tuple-element.9) | data formatting | bytes 331776
where the time goes:
time: 78.6 us; the launch traced here: 78.4 us
  Pallas kernels  74.4 us (95%)
  local copies, waits for them, and re-layouts  3.39 us (4%)
    pallas_call x1, Pallas kernels, body(): pl.pallas_call(kernel, out_shape=(jax.ShapeDtypeStruct((2, 64, D), BF16),...  74.4 us
    unnamed x2, local copies, waits for them, and re-layouts  3.39 us

commit v1 on v0

--- a/solution.py
+++ b/solution.py
@@ -117,17 +117,19 @@
         lo, hi, a, b = HEAD_WINDOWS[h]
         lanes = jnp.where(lane_mask(lo, hi, a, b), 1.0, 0.0).astype(BF16)
         q = qkv[:, a:b] * lanes
-        dq = dqkv[:, a:b] * lanes
+        both = jnp.concatenate([q, dqkv[:, a:b] * lanes], axis=0)
         k, dk = kx[:, a:b], dkx[:, a:b]
         v, dv = qkv[:, 1152 + a : 1152 + b], dqkv[:, 1152 + a : 1152 + b]
-        e = jnp.where(mask, jnp.exp(nt(q, k) * SCALE), 0.0)
+        against_k = nt(both, k)
+        e = jnp.where(mask, jnp.exp(against_k[:128] * SCALE), 0.0)
         pn = e * (1.0 / jnp.sum(e, axis=1, keepdims=True))
         pn_ref[h] = pn
         p = pn.astype(BF16)
-        ds = (nt(dq, k) + nt(q, dk)) * SCALE
+        ds = (against_k[128:] + nt(q, dk)) * SCALE
         dp = (pn * (ds - jnp.sum(pn * ds, axis=1, keepdims=True))).astype(BF16)
-        add_head(out, h, nn(p, v))
-        add_head(tan, h, nn(dp, v) + nn(p, dv))
+        against_v = nn(jnp.concatenate([p, dp], axis=0), v)
+        add_head(out, h, against_v[:128])
+        add_head(tan, h, against_v[128:] + nn(p, dv))
     return jnp.concatenate(out, axis=1), jnp.concatenate(tan, axis=1)
 
 
@@ -200,7 +202,9 @@
         scratch["r_" + name] = v((256, width), BF16)
     for i, (_, n, _, _) in enumerate(JOBS):
         scratch[f"p{i}"] = v((4, 144, n), BF16)
-        scratch[f"v{i}"] = v((3, 144, n), BF16)
+        scratch[f"u{i}"] = v((144, n), BF16)
+        scratch[f"m{i}"] = v((144, n), BF16)
+        scratch[f"v{i}"] = v((2, 144, n), BF16)
         scratch[f"s2_{i}"] = v((4, 48, n), BF16)
         scratch[f"v2_{i}"] = v((3, 48, n), BF16)
         scratch[f"s3_{i}"] = v((4, 16, n), BF16)
@@ -214,8 +218,8 @@
     scratch["a_recv"] = dma((4, 7))
     scratch["c_send"] = dma((len(LEFTS) + len(RIGHTS),))
     scratch["c_recv"] = dma((len(LEFTS) + len(RIGHTS),))
-    scratch["rs_send"] = dma((N_JOBS, 3, 3))
-    scratch["rs_recv"] = dma((N_JOBS, 3, 3))
+    scratch["rs_send"] = dma((N_JOBS, 12))
+    scratch["rs_recv"] = dma((N_JOBS, 12))
     return scratch
 
 
@@ -348,17 +352,19 @@
     s["r_o1"][0:128, :] = o1x
     share_right("o1")
     s_out, v_sout = s["wp"][:, S_OUT : S_OUT + OUT], s["wd"][:, S_OUT : S_OUT + OUT]
-    y = (clips_p + nt(o1x, s_out)).astype(BF16).astype(F32)
-    dy = (nt(do1x, s_out) + nt(o1x, v_sout)).astype(BF16).astype(F32)
+    through = nt(jnp.concatenate([o1x, do1x], axis=0), s_out)
+    y = (clips_p + through[:128]).astype(BF16).astype(F32)
+    dy = (through[128:] + nt(o1x, v_sout)).astype(BF16).astype(F32)
     h2f, rstd = norm_parts(y)
     h2 = h2f.astype(BF16)
-    dh2 = norm_tangent(h2f, rstd, dy).astype(BF16)
+    h2_both = jnp.concatenate([h2, norm_tangent(h2f, rstd, dy).astype(BF16)], axis=0)
     loaded(2)
     for lo in range(0, QKV, 256):
         wp = s["wp"][:, T_QKV + lo : T_QKV + lo + 256]
         wd = s["wd"][:, T_QKV + lo : T_QKV + lo + 256]
-        s["qkv2"][:, lo : lo + 256] = nn(h2, wp).astype(BF16)
-        s["dqkv2"][:, lo : lo + 256] = (nn(dh2, wp) + nn(h2, wd)).astype(BF16)
+        through = nn(h2_both, wp)
+        s["qkv2"][:, lo : lo + 256] = through[:128].astype(BF16)
+        s["dqkv2"][:, lo : lo + 256] = (through[128:] + nn(h2, wd)).astype(BF16)
     align_keys(s["qkv2"], s["kx2"])
     align_keys(s["dqkv2"], s["dkx"])
     o2, do2 = attend(s["qkv2"], s["dqkv2"], s["kx2"], s["dkx"], s["pn2"], same_patch)
@@ -379,82 +385,163 @@
     gy = (g.astype(F32) + norm_tangent(h2f, rstd, gh2)).astype(BF16)
     s["go_s"][...] = nn(gy, s_out).astype(BF16).reshape(8, 16, OUT)
     go_copies = frame_exchange(2, s["go_s"], s["go_r"])
+
+    s["pad2"][...] = jnp.zeros_like(s["pad2"])
+    s["pad3"][...] = jnp.zeros_like(s["pad3"])
+    flight = {}
+
+    def product(job):
+        _, n, axes, segments = JOBS[job]
+        needed = [name for _, _, terms in segments for left, right, _ in terms for name in (left, right)]
+        for name in needed:
+            copies = left_copies if name in left_copies else right_copies
+            if name not in shared:
+                copies[name].wait_recv()
+                shared.append(name)
+        part, first_in, ready = s[f"p{job}"], s[f"u{job}"], s[f"v{job}"]
+        for lo, hi, terms in segments:
+            acc = None
+            for left, right, at in terms:
+                term = nn(s["left"][LEFTS.index(left)], s["r_" + right][:, at : at + hi - lo])
+                acc = term if acc is None else acc + term
+            part[:, :, lo:hi] = acc.astype(BF16).reshape(4, 144, hi - lo)
+        here = where[axes[0]]
+        right, left = along(axes[0], 1), along(axes[0], 3)
+        ahead, behind, across = (here + 1) % 4, (here + 3) % 4, (here + 2) % 4
+        flight[job] = [
+            remote(src.at[pl.ds(at, rows)], dst.at[pl.ds(at, rows)], s["rs_send"].at[job, i], s["rs_recv"].at[job, i], to)
+            for i, (src, dst, at, rows, to) in enumerate(
+                [
+                    (part.at[across], first_in, 0, 80, right),
+                    (part.at[across], first_in, 80, 64, left),
+                    (part.at[ahead], ready.at[0], 80, 64, right),
+                    (part.at[behind], ready.at[1], 0, 80, left),
+                ]
+            )
+        ]
+
+    def merge(job):
+        here = where[JOBS[job][2][0]]
+        part, first_in, merged, ready = s[f"p{job}"], s[f"u{job}"], s[f"m{job}"], s[f"v{job}"]
+        for i, k, at, rows in [(0, 1, 0, 80), (1, 3, 80, 64)]:
+            flight[job][i].wait_recv()
+            own = part[(here + k) % 4, at : at + rows].astype(F32)
+            merged[at : at + rows] = (own + first_in[at : at + rows].astype(F32)).astype(BF16)
+            flight[job].append(
+                remote(
+                    merged.at[pl.ds(at, rows)],
+                    ready.at[i, pl.ds(at, rows)],
+                    s["rs_send"].at[job, 4 + i],
+                    s["rs_recv"].at[job, 4 + i],
+                    along(JOBS[job][2][0], k),
+                )
+            )
+
+    def scatter(job, stage, src, dst):
+        axis = JOBS[job][2][stage]
+        flight[job] = []
+        for k in (1, 2, 3):
+            i = 3 + 3 * stage + k - 1
+            flight[job].append(
+                remote(
+                    src.at[(where[axis] + k) % 4],
+                    dst.at[k - 1],
+                    s["rs_send"].at[job, i],
+                    s["rs_recv"].at[job, i],
+                    along(axis, k),
+                )
+            )
+
+    def second_stage(job):
+        _, n, axes, _ = JOBS[job]
+        arrived(flight[job][2:])
+        part, ready = s[f"p{job}"], s[f"v{job}"]
+        s["acc1"][:, :n] = part[where[axes[0]]].astype(F32) + ready[0].astype(F32) + ready[1].astype(F32)
+        for second in range(4):
+            for third in range(4):
+                at = second_rows(axes, second, third)
+                s["pad2"][9 * third : 9 * third + 9, :n] = s["acc1"][at : at + 9, :n]
+            s[f"s2_{job}"][second] = s["pad2"][:, :n].astype(BF16)
+        scatter(job, 1, s[f"s2_{job}"], s[f"v2_{job}"])
+
+    def total(job, stage, src, dst):
+        arrived(flight[job])
+        mine = src[where[JOBS[job][2][stage]]].astype(F32)
+        return mine + dst[0].astype(F32) + dst[1].astype(F32) + dst[2].astype(F32)
+
+    def third_stage(job):
+        n = JOBS[job][1]
+        s["acc2"][:, :n] = total(job, 1, s[f"s2_{job}"], s[f"v2_{job}"])
+        for third in range(4):
+            s["pad3"][0:9, :n] = s["acc2"][9 * third : 9 * third + 9, :n]
+            s[f"s3_{job}"][third] = s["pad3"][:, :n].astype(BF16)
+        scatter(job, 2, s[f"s3_{job}"], s[f"v3_{job}"])
+
+    def finish(job):
+        first, n, _, _ = JOBS[job]
+        gnv_ref[:, first : first + n] = total(job, 2, s[f"s3_{job}"], s[f"v3_{job}"])[0:9]
+
+    shared = []
+    prepare_left(h2.astype(F32), ["h2_y", "h2_x"])
+    prepare_left(g.astype(F32), ["g_x"])
+    product(1)
+    product(2)
+
+    arrived(go_copies)
+    s["go"][...] = left_64(s["go_r"][...].reshape(128, OUT).astype(F32)).astype(BF16)
+    attend_back(s["qkv1"], s["kx1"], s["pn1"], s["go"], s["r_q1"].at[pl.ds(0, 128)])
+    share_right("q1")
+
+    merge(1)
+    merge(2)
     prepare_left(gy.astype(F32), ["gy_z"])
-    prepare_left(h2.astype(F32), ["h2_z", "h2_y", "h2_x"])
-    prepare_left(g.astype(F32), ["g_x"])
-
+    prepare_left(h2.astype(F32), ["h2_z"])
+    product(0)
+    product(4)
+    product(5)
+    product(3)
     arrived(tan_copies)
     tan = s["tan_r"][...].reshape(128, D).astype(F32)
     for f in range(2):
         tan_ref[f] = jnp.concatenate(
             [tan[16 * t + 8 * f : 16 * t + 8 * f + 8] for t in range(8)], axis=0
         ).astype(BF16)
-    arrived(go_copies)
-    s["go"][...] = left_64(s["go_r"][...].reshape(128, OUT).astype(F32)).astype(BF16)
-    attend_back(s["qkv1"], s["kx1"], s["pn1"], s["go"], s["r_q1"].at[pl.ds(0, 128)])
-    share_right("q1")
-
-    for copy in left_copies.values():
-        copy.wait_recv()
-    for copy in right_copies.values():
-        copy.wait_recv()
-
-    def scatter(job, stage, src, dst):
-        axis = JOBS[job][2][stage]
-        copies = []
-        for k in (1, 2, 3):
-            t = (where[axis] + k) % 4
-            copies.append(
-                remote(
-                    src.at[t],
-                    dst.at[k - 1],
-                    s["rs_send"].at[job, stage, k - 1],
-                    s["rs_recv"].at[job, stage, k - 1],
-                    along(axis, k),
-                )
-            )
-        return copies
-
-    def total(job, stage, src, dst):
-        mine = src[where[JOBS[job][2][stage]]].astype(F32)
-        return mine + dst[0].astype(F32) + dst[1].astype(F32) + dst[2].astype(F32)
-
-    s["pad2"][...] = jnp.zeros_like(s["pad2"])
-    s["pad3"][...] = jnp.zeros_like(s["pad3"])
-    flight = []
-    for job, (_, n, _, segments) in enumerate(JOBS):
-        for lo, hi, terms in segments:
-            acc = None
-            for left, right, at in terms:
-                term = nn(s["left"][LEFTS.index(left)], s["r_" + right][:, at : at + hi - lo])
-                acc = term if acc is None else acc + term
-            s[f"p{job}"][:, :, lo:hi] = acc.astype(BF16).reshape(4, 144, hi - lo)
-        flight.append(scatter(job, 0, s[f"p{job}"], s[f"v{job}"]))
-
-    for job, (_, n, axes, _) in enumerate(JOBS):
-        arrived(flight[job])
-        s["acc1"][:, :n] = total(job, 0, s[f"p{job}"], s[f"v{job}"])
-        for second in range(4):
-            for third in range(4):
-                at = second_rows(axes, second, third)
-                s["pad2"][9 * third : 9 * third + 9, :n] = s["acc1"][at : at + 9, :n]
-            s[f"s2_{job}"][second] = s["pad2"][:, :n].astype(BF16)
-        flight[job] = scatter(job, 1, s[f"s2_{job}"], s[f"v2_{job}"])
-
-    for job, (_, n, _, _) in enumerate(JOBS):
-        arrived(flight[job])
-        s["acc2"][:, :n] = total(job, 1, s[f"s2_{job}"], s[f"v2_{job}"])
-        for third in range(4):
-            s["pad3"][0:9, :n] = s["acc2"][9 * third : 9 * third + 9, :n]
-            s[f"s3_{job}"][third] = s["pad3"][:, :n].astype(BF16)
-        flight[job] = scatter(job, 2, s[f"s3_{job}"], s[f"v3_{job}"])
-
-    for job, (first, n, _, _) in enumerate(JOBS):
-        arrived(flight[job])
-        gnv_ref[:, first : first + n] = total(job, 2, s[f"s3_{job}"], s[f"v3_{job}"])[0:9]
+    merge(0)
+    second_stage(1)
+    second_stage(2)
+    merge(4)
+    merge(5)
+    merge(3)
+    second_stage(0)
+    third_stage(1)
+    third_stage(2)
+    second_stage(4)
+    second_stage(5)
+    second_stage(3)
+    third_stage(0)
+    finish(1)
+    finish(2)
+    third_stage(4)
+    third_stage(5)
+    third_stage(3)
+    finish(0)
+    finish(4)
+    finish(5)
+    finish(3)
 
     for copy in sent:
         copy.wait_send()
+
+
+def place(tan_in, gnv_in, tan_out, gnv_out, sem):
+    copies = [
+        pltpu.make_async_copy(tan_in, tan_out, sem.at[0]),
+        pltpu.make_async_copy(gnv_in, gnv_out, sem.at[1]),
+    ]
+    for copy in copies:
+        copy.start()
+    for copy in copies:
+        copy.wait()
 
 
 def body(clips, params, direction):
@@ -475,6 +562,16 @@
             collective_id=0, has_side_effects=True, vmem_limit_bytes=62 * 2**20
         ),
     )(clips[0], params, direction)
+    tangent, gnv = pl.pallas_call(
+        place,
+        out_shape=(
+            jax.ShapeDtypeStruct((2, 64, D), BF16),
+            jax.ShapeDtypeStruct((9, 4608), F32),
+        ),
+        in_specs=[pl.BlockSpec(memory_space=pl.ANY)] * 2,
+        out_specs=(pl.BlockSpec(memory_space=pl.ANY),) * 2,
+        scratch_shapes=[pltpu.SemaphoreType.DMA((2,))],
+    )(tangent, gnv)
     return tangent[None], gnv
 
 

time: 78.6 us -> 94 us (1.20)
  Pallas kernels: 74.4 us -> 92.4 us
  local copies, waits for them, and re-layouts: 3.39 us -> 0 us
    pallas_call x0 -> x1, Pallas kernels: none -> 19 us  [body(): pl.pallas_call(place, out_shape=(jax.ShapeDtypeStruct((2, 64, D), BF16),...]
    unnamed x2 -> x0, local copies, waits for them, and re-layouts: 3.39 us -> none
where the time goes in v1:
time: 94 us; the launch traced here: 93.2 us
  Pallas kernels  92.4 us (98%)
    pallas_call x1, Pallas kernels, body(): pl.pallas_call(kernel, out_shape=(jax.ShapeDtypeStruct((2, 64, D), BF16),...  73.4 us
    pallas_call x1, Pallas kernels, body(): pl.pallas_call(place, out_shape=(jax.ShapeDtypeStruct((2, 64, D), BF16),...  19 us

profile of v1, /device:TPU:1, one launch (start us, length us, event | category | flops | bytes accessed | tf_op | source)
XLA Modules:
  0.0 93.2 jit_solution(9492487131601465418)
XLA Ops:
  0.6 73.4 %shard_map.50 = (bf16[2,64,1152]{2,1,0:T(8,128)(2,1)}, f32[9,4608]{1,0:T(8,128)}) custom-call(bf16[2,64,1152]{2,1,0:T(8,128)(2,1)} %bitcast.2, bf16[1152,4608]{1,0:T(8,128)(2,1)} %params_ref.1, bf16[1152,4608]{1,0:T(8,128)(2,1)} %direction_ref.1), custom_call_target="tpu_custom_call" | custom-call | tf_op jit(solution)/shard_map/pallas_call | solution.py:548
  74.1 19.0 %shard_map.51 = (bf16[2,64,1152]{2,1,0:T(8,128)(2,1)}, f32[9,4608]{1,0:T(8,128)}) custom-call(bf16[2,64,1152]{2,1,0:T(8,128)(2,1)} %get-tuple-element.6.tan_in, f32[9,4608]{1,0:T(8,128)} %get-tuple-element.7.gnv_in), custom_call_target="tpu_custom_call" | custom-call | tf_op jit(solution)/shard_map/pallas_call | solution.py:565

commit v2 on v1

--- a/solution.py
+++ b/solution.py
@@ -111,7 +111,16 @@
         tiles[j] = jnp.where(mask, piece, old)
 
 
-def attend(qkv, dqkv, kx, dkx, pn_ref, mask):
+def first_part(tiles):
+    moved = right_64(jnp.concatenate(tiles[:3], axis=1))
+    return jnp.where(lane_mask(64, 384, 0, 384), moved, 0.0).astype(BF16)
+
+
+def second_part(tiles):
+    return left_64(jnp.concatenate(tiles[2:], axis=1))[:, :256].astype(BF16)
+
+
+def attend(qkv, dqkv, kx, dkx, pn_ref, mask, after_head_4):
     out, tan = [None] * 5, [None] * 5
     for h in range(HEADS):
         lo, hi, a, b = HEAD_WINDOWS[h]
@@ -130,7 +139,9 @@
         against_v = nn(jnp.concatenate([p, dp], axis=0), v)
         add_head(out, h, against_v[:128])
         add_head(tan, h, against_v[128:] + nn(p, dv))
-    return jnp.concatenate(out, axis=1), jnp.concatenate(tan, axis=1)
+        if h == 4:
+            after_head_4(out, tan)
+    return out, tan
 
 
 def attend_back(qkv, kx, pn_ref, go, grad_ref):
@@ -187,8 +198,10 @@
         "go": v((128, OUT), BF16),
         "clips_s": v((8, 16, D), BF16),
         "clips_r": v((8, 16, D), BF16),
-        "attn_s": v((8, 16, 2 * OUT), BF16),
-        "attn_r": v((8, 16, 2 * OUT), BF16),
+        "attn_s": v((8, 16, 768), BF16),
+        "attn_r": v((8, 16, 768), BF16),
+        "attn2_s": v((8, 16, 512), BF16),
+        "attn2_r": v((8, 16, 512), BF16),
         "go_s": v((8, 16, OUT), BF16),
         "go_r": v((8, 16, OUT), BF16),
         "tan_s": v((8, 16, D), BF16),
@@ -214,8 +227,8 @@
     scratch["pad2"] = v((48, 1024), F32)
     scratch["pad3"] = v((16, 1024), F32)
     scratch["w_sem"] = dma((8,))
-    scratch["a_send"] = dma((4, 7))
-    scratch["a_recv"] = dma((4, 7))
+    scratch["a_send"] = dma((5, 7))
+    scratch["a_recv"] = dma((5, 7))
     scratch["c_send"] = dma((len(LEFTS) + len(RIGHTS),))
     scratch["c_recv"] = dma((len(LEFTS) + len(RIGHTS),))
     scratch["rs_send"] = dma((N_JOBS, 12))
@@ -336,10 +349,17 @@
     same_patch = row % 8 == col % 8
     align_keys(s["qkv1"], s["kx1"])
     align_keys(s["dqkv1"], s["dkx"])
-    o1, do1 = attend(s["qkv1"], s["dqkv1"], s["kx1"], s["dkx"], s["pn1"], same_frame)
-    s["attn_s"][:, :, 0:OUT] = right_64(o1).astype(BF16).reshape(8, 16, OUT)
-    s["attn_s"][:, :, OUT:] = right_64(do1).astype(BF16).reshape(8, 16, OUT)
-    attn_copies = frame_exchange(1, s["attn_s"], s["attn_r"])
+    attn_copies = []
+
+    def send_first(out, tan):
+        s["attn_s"][:, :, 0:384] = first_part(out).reshape(8, 16, 384)
+        s["attn_s"][:, :, 384:768] = first_part(tan).reshape(8, 16, 384)
+        attn_copies.extend(frame_exchange(1, s["attn_s"], s["attn_r"]))
+
+    o1, do1 = attend(s["qkv1"], s["dqkv1"], s["kx1"], s["dkx"], s["pn1"], same_frame, send_first)
+    s["attn2_s"][:, :, 0:256] = second_part(o1).reshape(8, 16, 256)
+    s["attn2_s"][:, :, 256:512] = second_part(do1).reshape(8, 16, 256)
+    attn_copies.extend(frame_exchange(4, s["attn2_s"], s["attn2_r"]))
 
     prepare_left(h1f.astype(BF16).astype(F32), ["h1_z", "h1_y", "h1_x"])
 
@@ -347,8 +367,9 @@
     loaded(1)
     arrived(attn_copies)
     clips_p = s["clips_r"][...].reshape(128, D).astype(F32)
-    o1x = s["attn_r"][:, :, 0:OUT].reshape(128, OUT)
-    do1x = s["attn_r"][:, :, OUT:].reshape(128, OUT)
+    parts = s["attn_r"][...].reshape(128, 768), s["attn2_r"][...].reshape(128, 512)
+    o1x = jnp.concatenate([parts[0][:, :384], parts[1][:, :256]], axis=1)
+    do1x = jnp.concatenate([parts[0][:, 384:], parts[1][:, 256:]], axis=1)
     s["r_o1"][0:128, :] = o1x
     share_right("o1")
     s_out, v_sout = s["wp"][:, S_OUT : S_OUT + OUT], s["wd"][:, S_OUT : S_OUT + OUT]
@@ -367,8 +388,9 @@
         s["dqkv2"][:, lo : lo + 256] = (through[128:] + nn(h2, wd)).astype(BF16)
     align_keys(s["qkv2"], s["kx2"])
     align_keys(s["dqkv2"], s["dkx"])
-    o2, do2 = attend(s["qkv2"], s["dqkv2"], s["kx2"], s["dkx"], s["pn2"], same_patch)
-    o2x, do2x = right_64(o2).astype(BF16), right_64(do2).astype(BF16)
+    o2, do2 = attend(s["qkv2"], s["dqkv2"], s["kx2"], s["dkx"], s["pn2"], same_patch, lambda *_: None)
+    o2x = right_64(jnp.concatenate(o2, axis=1)).astype(BF16)
+    do2x = right_64(jnp.concatenate(do2, axis=1)).astype(BF16)
     s["r_o2"][0:128, :] = o2x
     share_right("o2")
     loaded(3)
@@ -482,10 +504,12 @@
         gnv_ref[:, first : first + n] = total(job, 2, s[f"s3_{job}"], s[f"v3_{job}"])[0:9]
 
     shared = []
-    prepare_left(h2.astype(F32), ["h2_y", "h2_x"])
+    prepare_left(gy.astype(F32), ["gy_z"])
+    prepare_left(h2.astype(F32), ["h2_y", "h2_x", "h2_z"])
     prepare_left(g.astype(F32), ["g_x"])
     product(1)
     product(2)
+    product(0)
 
     arrived(go_copies)
     s["go"][...] = left_64(s["go_r"][...].reshape(128, OUT).astype(F32)).astype(BF16)
@@ -494,9 +518,7 @@
 
     merge(1)
     merge(2)
-    prepare_left(gy.astype(F32), ["gy_z"])
-    prepare_left(h2.astype(F32), ["h2_z"])
-    product(0)
+    merge(0)
     product(4)
     product(5)
     product(3)
@@ -506,25 +528,24 @@
         tan_ref[f] = jnp.concatenate(
             [tan[16 * t + 8 * f : 16 * t + 8 * f + 8] for t in range(8)], axis=0
         ).astype(BF16)
-    merge(0)
     second_stage(1)
     second_stage(2)
+    second_stage(0)
     merge(4)
     merge(5)
     merge(3)
-    second_stage(0)
     third_stage(1)
     third_stage(2)
+    third_stage(0)
     second_stage(4)
     second_stage(5)
     second_stage(3)
-    third_stage(0)
     finish(1)
     finish(2)
+    finish(0)
     third_stage(4)
     third_stage(5)
     third_stage(3)
-    finish(0)
     finish(4)
     finish(5)
     finish(3)
@@ -533,15 +554,9 @@
         copy.wait_send()
 
 
-def place(tan_in, gnv_in, tan_out, gnv_out, sem):
-    copies = [
-        pltpu.make_async_copy(tan_in, tan_out, sem.at[0]),
-        pltpu.make_async_copy(gnv_in, gnv_out, sem.at[1]),
-    ]
-    for copy in copies:
-        copy.start()
-    for copy in copies:
-        copy.wait()
+def place(tan_in, gnv_in, tan_out, gnv_out):
+    tan_out[...] = tan_in[...]
+    gnv_out[...] = gnv_in[...]
 
 
 def body(clips, params, direction):
@@ -568,9 +583,8 @@
             jax.ShapeDtypeStruct((2, 64, D), BF16),
             jax.ShapeDtypeStruct((9, 4608), F32),
         ),
-        in_specs=[pl.BlockSpec(memory_space=pl.ANY)] * 2,
-        out_specs=(pl.BlockSpec(memory_space=pl.ANY),) * 2,
-        scratch_shapes=[pltpu.SemaphoreType.DMA((2,))],
+        in_specs=[pl.BlockSpec(memory_space=pltpu.VMEM)] * 2,
+        out_specs=(pl.BlockSpec(memory_space=pltpu.VMEM),) * 2,
     )(tangent, gnv)
     return tangent[None], gnv
 

time: 94 us -> 69.5 us (0.74)
  Pallas kernels: 92.4 us -> 68.6 us
    pallas_call x1, Pallas kernels: 19 us -> 1.88 us  [body(): pl.pallas_call(place, out_shape=(jax.ShapeDtypeStruct((2, 64, D), BF16),...]
    pallas_call x1, Pallas kernels: 73.4 us -> 66.7 us  [body(): pl.pallas_call(kernel, out_shape=(jax.ShapeDtypeStruct((2, 64, D), BF16),...]
where the time goes in v2:
time: 69.5 us; the launch traced here: 69.2 us
  Pallas kernels  68.6 us (99%)
    pallas_call x1, Pallas kernels, body(): pl.pallas_call(kernel, out_shape=(jax.ShapeDtypeStruct((2, 64, D), BF16),...  66.7 us
    pallas_call x1, Pallas kernels, body(): pl.pallas_call(place, out_shape=(jax.ShapeDtypeStruct((2, 64, D), BF16),...  1.88 us

profile of v2, /device:TPU:1, one launch (start us, length us, event | category | flops | bytes accessed | tf_op | source)
XLA Modules:
  0.0 69.2 jit_solution(5919933843502628020)
XLA Ops:
  0.6 66.7 %shard_map.50 = (bf16[2,64,1152]{2,1,0:T(8,128)(2,1)}, f32[9,4608]{1,0:T(8,128)}) custom-call(bf16[2,64,1152]{2,1,0:T(8,128)(2,1)} %bitcast.2, bf16[1152,4608]{1,0:T(8,128)(2,1)} %params_ref.1, bf16[1152,4608]{1,0:T(8,128)(2,1)} %direction_ref.1), custom_call_target="tpu_custom_call" | custom-call | tf_op jit(solution)/shard_map/pallas_call | solution.py:563
  67.3 1.9 %shard_map.51 = (bf16[2,64,1152]{2,1,0:T(8,128)(2,1)}, f32[9,4608]{1,0:T(8,128)}) custom-call(bf16[2,64,1152]{2,1,0:T(8,128)(2,1)} %get-tuple-element.6.tan_in, f32[9,4608]{1,0:T(8,128)} %get-tuple-element.7.gnv_in), custom_call_target="tpu_custom_call" | custom-call | tf_op jit(solution)/shard_map/pallas_call | solution.py:580

commit v3 on v2

--- a/solution.py
+++ b/solution.py
@@ -23,22 +23,19 @@
     for h in range(HEADS)
 ]
 
-LEFTS = ["gy_z", "h2_z", "h2_y", "h2_x", "g_x", "h1_z", "h1_y", "h1_x"]
+LEFTS = ["g_z", "g_x", "h2_y", "h2_x", "gy_z", "h1_z", "h1_y", "h1_x"]
 RIGHTS = {"q1": QKV, "o1": OUT, "q2": QKV, "o2": OUT}
 
 JOBS = [
-    (14 * 128, 1024, "zxy", [(0, 512, [("gy_z", "o1", 128)]), (512, 1024, [("h2_z", "q2", 0)])]),
-    (22 * 128, 896, "yzx", [(0, 896, [("h2_y", "q2", 512)])]),
+    (32 * 128, 512, "zxy", [(0, 512, [("g_z", "o2", 128)])]),
+    (18 * 128, 896, "yzx", [(0, 896, [("h2_y", "q2", 0)])]),
     (
-        29 * 128,
+        25 * 128,
         896,
         "xyz",
-        [
-            (0, 256, [("h2_x", "q2", 1408)]),
-            (256, 384, [("h2_x", "q2", 1664), ("g_x", "o2", 0)]),
-            (384, 896, [("g_x", "o2", 128)]),
-        ],
+        [(0, 768, [("h2_x", "q2", 896)]), (768, 896, [("h2_x", "q2", 1664), ("g_x", "o2", 0)])],
     ),
+    (14 * 128, 512, "zxy", [(0, 512, [("gy_z", "o1", 128)])]),
     (
         10 * 128,
         512,
@@ -49,6 +46,10 @@
     (0, 640, "xyz", [(0, 640, [("h1_x", "q1", 0)])]),
 ]
 N_JOBS = len(JOBS)
+
+
+def third_width(n):
+    return (n // 128 + 2) // 2 * 128
 
 
 def row_moves(order):
@@ -144,7 +145,7 @@
     return out, tan
 
 
-def attend_back(qkv, kx, pn_ref, go, grad_ref):
+def attend_back(qkv, kx, pn_ref, go, grad_ref, after_head_4):
     gq, gk, gv = [None] * 5, [None] * 5, [None] * 5
     for h in range(HEADS):
         lo, hi, a, b = HEAD_WINDOWS[h]
@@ -156,6 +157,8 @@
         add_head(gq, h, nn(gs, kx[:, a:b]))
         add_head(gk, h, tn(gs, qkv[:, a:b]))
         add_head(gv, h, tn(pn.astype(BF16), gow))
+        if h == 4:
+            after_head_4()
     gkr = right_64(jnp.concatenate(gk, axis=1))
     for j in range(4):
         grad_ref[:, j * 128 : (j + 1) * 128] = gq[j].astype(BF16)
@@ -218,14 +221,15 @@
         scratch[f"u{i}"] = v((144, n), BF16)
         scratch[f"m{i}"] = v((144, n), BF16)
         scratch[f"v{i}"] = v((2, 144, n), BF16)
-        scratch[f"s2_{i}"] = v((4, 48, n), BF16)
-        scratch[f"v2_{i}"] = v((3, 48, n), BF16)
-        scratch[f"s3_{i}"] = v((4, 16, n), BF16)
-        scratch[f"v3_{i}"] = v((3, 16, n), BF16)
-    scratch["acc1"] = v((144, 1024), F32)
-    scratch["acc2"] = v((48, 1024), F32)
-    scratch["pad2"] = v((48, 1024), F32)
-    scratch["pad3"] = v((16, 1024), F32)
+        scratch[f"s2_{i}"] = v((4, 32, n + 128), BF16)
+        scratch[f"v2_{i}"] = v((3, 32, n + 128), BF16)
+        scratch[f"s3_{i}"] = v((4, 16, third_width(n)), BF16)
+        scratch[f"v3_{i}"] = v((3, 16, third_width(n)), BF16)
+    scratch["acc1"] = v((144, 896), F32)
+    scratch["acc2"] = v((40, 896), F32)
+    scratch["pad2"] = v((40, 896), F32)
+    scratch["ext2"] = v((32, 128), F32)
+    scratch["pad3"] = v((16, 512), F32)
     scratch["w_sem"] = dma((8,))
     scratch["a_send"] = dma((5, 7))
     scratch["a_recv"] = dma((5, 7))
@@ -335,82 +339,10 @@
             ref.at[pl.ds(0, 128)], ref.at[pl.ds(128, 128)], s["c_send"].at[i], s["c_recv"].at[i], partner
         )
 
-    loaded(0)
-    for lo in range(0, QKV, 256):
-        s["qkv1"][:, lo : lo + 256] = nn(s["h1"][...], s["wp"][:, lo : lo + 256]).astype(BF16)
-        s["dqkv1"][:, lo : lo + 256] = nn(s["h1"][...], s["wd"][:, lo : lo + 256]).astype(BF16)
-
-    def align_keys(qkv, kx):
-        kx[...] = left_64(qkv[:, 512:1152].astype(F32)).astype(BF16)
-
-    row = lax.broadcasted_iota(jnp.int32, (128, 128), 0)
-    col = lax.broadcasted_iota(jnp.int32, (128, 128), 1)
-    same_frame = row // 8 % 2 == col // 8 % 2
-    same_patch = row % 8 == col % 8
-    align_keys(s["qkv1"], s["kx1"])
-    align_keys(s["dqkv1"], s["dkx"])
-    attn_copies = []
-
-    def send_first(out, tan):
-        s["attn_s"][:, :, 0:384] = first_part(out).reshape(8, 16, 384)
-        s["attn_s"][:, :, 384:768] = first_part(tan).reshape(8, 16, 384)
-        attn_copies.extend(frame_exchange(1, s["attn_s"], s["attn_r"]))
-
-    o1, do1 = attend(s["qkv1"], s["dqkv1"], s["kx1"], s["dkx"], s["pn1"], same_frame, send_first)
-    s["attn2_s"][:, :, 0:256] = second_part(o1).reshape(8, 16, 256)
-    s["attn2_s"][:, :, 256:512] = second_part(do1).reshape(8, 16, 256)
-    attn_copies.extend(frame_exchange(4, s["attn2_s"], s["attn2_r"]))
-
-    prepare_left(h1f.astype(BF16).astype(F32), ["h1_z", "h1_y", "h1_x"])
-
-    arrived(clips_copies)
-    loaded(1)
-    arrived(attn_copies)
-    clips_p = s["clips_r"][...].reshape(128, D).astype(F32)
-    parts = s["attn_r"][...].reshape(128, 768), s["attn2_r"][...].reshape(128, 512)
-    o1x = jnp.concatenate([parts[0][:, :384], parts[1][:, :256]], axis=1)
-    do1x = jnp.concatenate([parts[0][:, 384:], parts[1][:, 256:]], axis=1)
-    s["r_o1"][0:128, :] = o1x
-    share_right("o1")
-    s_out, v_sout = s["wp"][:, S_OUT : S_OUT + OUT], s["wd"][:, S_OUT : S_OUT + OUT]
-    through = nt(jnp.concatenate([o1x, do1x], axis=0), s_out)
-    y = (clips_p + through[:128]).astype(BF16).astype(F32)
-    dy = (through[128:] + nt(o1x, v_sout)).astype(BF16).astype(F32)
-    h2f, rstd = norm_parts(y)
-    h2 = h2f.astype(BF16)
-    h2_both = jnp.concatenate([h2, norm_tangent(h2f, rstd, dy).astype(BF16)], axis=0)
-    loaded(2)
-    for lo in range(0, QKV, 256):
-        wp = s["wp"][:, T_QKV + lo : T_QKV + lo + 256]
-        wd = s["wd"][:, T_QKV + lo : T_QKV + lo + 256]
-        through = nn(h2_both, wp)
-        s["qkv2"][:, lo : lo + 256] = through[:128].astype(BF16)
-        s["dqkv2"][:, lo : lo + 256] = (through[128:] + nn(h2, wd)).astype(BF16)
-    align_keys(s["qkv2"], s["kx2"])
-    align_keys(s["dqkv2"], s["dkx"])
-    o2, do2 = attend(s["qkv2"], s["dqkv2"], s["kx2"], s["dkx"], s["pn2"], same_patch, lambda *_: None)
-    o2x = right_64(jnp.concatenate(o2, axis=1)).astype(BF16)
-    do2x = right_64(jnp.concatenate(do2, axis=1)).astype(BF16)
-    s["r_o2"][0:128, :] = o2x
-    share_right("o2")
-    loaded(3)
-    t_out, v_tout = s["wp"][:, T_OUT : T_OUT + OUT], s["wd"][:, T_OUT : T_OUT + OUT]
-    tangent = (dy + nt(do2x, t_out) + nt(o2x, v_tout)).astype(BF16)
-    s["tan_s"][...] = tangent.reshape(8, 16, D)
-    tan_copies = frame_exchange(3, s["tan_s"], s["tan_r"])
-    g = (tangent.astype(F32) * (16384 ** (-0.5))).astype(BF16)
-    s["go"][...] = left_64(nn(g, t_out)).astype(BF16)
-    attend_back(s["qkv2"], s["kx2"], s["pn2"], s["go"], s["r_q2"].at[pl.ds(0, 128)])
-    share_right("q2")
-    gq2 = s["r_q2"][0:128, :]
-    gh2 = nt(gq2, s["wp"][:, T_QKV : T_QKV + QKV])
-    gy = (g.astype(F32) + norm_tangent(h2f, rstd, gh2)).astype(BF16)
-    s["go_s"][...] = nn(gy, s_out).astype(BF16).reshape(8, 16, OUT)
-    go_copies = frame_exchange(2, s["go_s"], s["go_r"])
-
-    s["pad2"][...] = jnp.zeros_like(s["pad2"])
+    s["ext2"][...] = jnp.zeros_like(s["ext2"])
     s["pad3"][...] = jnp.zeros_like(s["pad3"])
     flight = {}
+    shared = []
 
     def product(job):
         _, n, axes, segments = JOBS[job]
@@ -483,7 +415,10 @@
             for third in range(4):
                 at = second_rows(axes, second, third)
                 s["pad2"][9 * third : 9 * third + 9, :n] = s["acc1"][at : at + 9, :n]
-            s[f"s2_{job}"][second] = s["pad2"][:, :n].astype(BF16)
+            for j in range(n // 128):
+                s["ext2"][4 * j : 4 * j + 4] = s["pad2"][32:36, 128 * j : 128 * j + 128]
+            s[f"s2_{job}"][second, :, :n] = s["pad2"][0:32, :n].astype(BF16)
+            s[f"s2_{job}"][second, :, n:] = s["ext2"][...].astype(BF16)
         scatter(job, 1, s[f"s2_{job}"], s[f"v2_{job}"])
 
     def total(job, stage, src, dst):
@@ -493,62 +428,145 @@
 
     def third_stage(job):
         n = JOBS[job][1]
-        s["acc2"][:, :n] = total(job, 1, s[f"s2_{job}"], s[f"v2_{job}"])
+        tiles, width = n // 128, third_width(n)
+        sums = total(job, 1, s[f"s2_{job}"], s[f"v2_{job}"])
+        s["acc2"][0:32, :n] = sums[:, :n]
+        s["ext2"][...] = sums[:, n:]
+        for j in range(tiles):
+            s["acc2"][32:36, 128 * j : 128 * j + 128] = s["ext2"][4 * j : 4 * j + 4]
         for third in range(4):
-            s["pad3"][0:9, :n] = s["acc2"][9 * third : 9 * third + 9, :n]
-            s[f"s3_{job}"][third] = s["pad3"][:, :n].astype(BF16)
+            for j in range(tiles):
+                lanes, at, ninth = slice(128 * j, 128 * j + 128), 128 * (j // 2), 128 * (tiles // 2)
+                s["pad3"][8 * (j % 2) : 8 * (j % 2) + 8, at : at + 128] = s["acc2"][9 * third : 9 * third + 8, lanes]
+                row = 8 * (tiles % 2) + j
+                s["pad3"][row : row + 1, ninth : ninth + 128] = s["acc2"][9 * third + 8 : 9 * third + 9, lanes]
+            s[f"s3_{job}"][third] = s["pad3"][:, :width].astype(BF16)
         scatter(job, 2, s[f"s3_{job}"], s[f"v3_{job}"])
 
     def finish(job):
         first, n, _, _ = JOBS[job]
-        gnv_ref[:, first : first + n] = total(job, 2, s[f"s3_{job}"], s[f"v3_{job}"])[0:9]
-
-    shared = []
+        tiles, width = n // 128, third_width(n)
+        s["pad3"][:, :width] = total(job, 2, s[f"s3_{job}"], s[f"v3_{job}"])
+        for j in range(tiles):
+            lanes, at, ninth = slice(first + 128 * j, first + 128 * j + 128), 128 * (j // 2), 128 * (tiles // 2)
+            row = 8 * (tiles % 2) + j
+            gnv_ref[0:8, lanes] = s["pad3"][8 * (j % 2) : 8 * (j % 2) + 8, at : at + 128]
+            gnv_ref[8:9, lanes] = s["pad3"][row : row + 1, ninth : ninth + 128]
+
+    loaded(0)
+    for lo in range(0, QKV, 256):
+        s["qkv1"][:, lo : lo + 256] = nn(s["h1"][...], s["wp"][:, lo : lo + 256]).astype(BF16)
+        s["dqkv1"][:, lo : lo + 256] = nn(s["h1"][...], s["wd"][:, lo : lo + 256]).astype(BF16)
+
+    def align_keys(qkv, kx):
+        kx[...] = left_64(qkv[:, 512:1152].astype(F32)).astype(BF16)
+
+    row = lax.broadcasted_iota(jnp.int32, (128, 128), 0)
+    col = lax.broadcasted_iota(jnp.int32, (128, 128), 1)
+    same_frame = row // 8 % 2 == col // 8 % 2
+    same_patch = row % 8 == col % 8
+    align_keys(s["qkv1"], s["kx1"])
+    align_keys(s["dqkv1"], s["dkx"])
+    attn_copies = []
+
+    def send_first(out, tan):
+        s["attn_s"][:, :, 0:384] = first_part(out).reshape(8, 16, 384)
+        s["attn_s"][:, :, 384:768] = first_part(tan).reshape(8, 16, 384)
+        attn_copies.extend(frame_exchange(1, s["attn_s"], s["attn_r"]))
+
+    o1, do1 = attend(s["qkv1"], s["dqkv1"], s["kx1"], s["dkx"], s["pn1"], same_frame, send_first)
+    s["attn2_s"][:, :, 0:256] = second_part(o1).reshape(8, 16, 256)
+    s["attn2_s"][:, :, 256:512] = second_part(do1).reshape(8, 16, 256)
+    attn_copies.extend(frame_exchange(4, s["attn2_s"], s["attn2_r"]))
+
+    prepare_left(h1f.astype(BF16).astype(F32), ["h1_z", "h1_y", "h1_x"])
+
+    arrived(clips_copies)
+    loaded(1)
+    arrived(attn_copies)
+    clips_p = s["clips_r"][...].reshape(128, D).astype(F32)
+    parts = s["attn_r"][...].reshape(128, 768), s["attn2_r"][...].reshape(128, 512)
+    o1x = jnp.concatenate([parts[0][:, :384], parts[1][:, :256]], axis=1)
+    do1x = jnp.concatenate([parts[0][:, 384:], parts[1][:, 256:]], axis=1)
+    s["r_o1"][0:128, :] = o1x
+    share_right("o1")
+    s_out, v_sout = s["wp"][:, S_OUT : S_OUT + OUT], s["wd"][:, S_OUT : S_OUT + OUT]
+    through = nt(jnp.concatenate([o1x, do1x], axis=0), s_out)
+    y = (clips_p + through[:128]).astype(BF16).astype(F32)
+    dy = (through[128:] + nt(o1x, v_sout)).astype(BF16).astype(F32)
+    h2f, rstd = norm_parts(y)
+    h2 = h2f.astype(BF16)
+    h2_both = jnp.concatenate([h2, norm_tangent(h2f, rstd, dy).astype(BF16)], axis=0)
+    prepare_left(h2.astype(F32), ["h2_y", "h2_x"])
+    loaded(2)
+    for lo in range(0, QKV, 256):
+        wp = s["wp"][:, T_QKV + lo : T_QKV + lo + 256]
+        wd = s["wd"][:, T_QKV + lo : T_QKV + lo + 256]
+        through = nn(h2_both, wp)
+        s["qkv2"][:, lo : lo + 256] = through[:128].astype(BF16)
+        s["dqkv2"][:, lo : lo + 256] = (through[128:] + nn(h2, wd)).astype(BF16)
+    align_keys(s["qkv2"], s["kx2"])
+    align_keys(s["dqkv2"], s["dkx"])
+    o2, do2 = attend(s["qkv2"], s["dqkv2"], s["kx2"], s["dkx"], s["pn2"], same_patch, lambda *_: None)
+    o2x = right_64(jnp.concatenate(o2, axis=1)).astype(BF16)
+    do2x = right_64(jnp.concatenate(do2, axis=1)).astype(BF16)
+    s["r_o2"][0:128, :] = o2x
+    share_right("o2")
+    loaded(3)
+    t_out, v_tout = s["wp"][:, T_OUT : T_OUT + OUT], s["wd"][:, T_OUT : T_OUT + OUT]
+    tangent = (dy + nt(do2x, t_out) + nt(o2x, v_tout)).astype(BF16)
+    s["tan_s"][...] = tangent.reshape(8, 16, D)
+    tan_copies = frame_exchange(3, s["tan_s"], s["tan_r"])
+    g = (tangent.astype(F32) * (16384 ** (-0.5))).astype(BF16)
+    prepare_left(g.astype(F32), ["g_z", "g_x"])
+    s["go"][...] = left_64(nn(g, t_out)).astype(BF16)
+    attend_back(s["qkv2"], s["kx2"], s["pn2"], s["go"], s["r_q2"].at[pl.ds(0, 128)], lambda: product(0))
+    share_right("q2")
+    gq2 = s["r_q2"][0:128, :]
+    gh2 = nt(gq2, s["wp"][:, T_QKV : T_QKV + QKV])
+    gy = (g.astype(F32) + norm_tangent(h2f, rstd, gh2)).astype(BF16)
+    s["go_s"][...] = nn(gy, s_out).astype(BF16).reshape(8, 16, OUT)
+    go_copies = frame_exchange(2, s["go_s"], s["go_r"])
+
     prepare_left(gy.astype(F32), ["gy_z"])
-    prepare_left(h2.astype(F32), ["h2_y", "h2_x", "h2_z"])
-    prepare_left(g.astype(F32), ["g_x"])
     product(1)
     product(2)
-    product(0)
+    product(3)
+    merge(0)
 
     arrived(go_copies)
     s["go"][...] = left_64(s["go_r"][...].reshape(128, OUT).astype(F32)).astype(BF16)
-    attend_back(s["qkv1"], s["kx1"], s["pn1"], s["go"], s["r_q1"].at[pl.ds(0, 128)])
+    attend_back(s["qkv1"], s["kx1"], s["pn1"], s["go"], s["r_q1"].at[pl.ds(0, 128)], lambda: None)
     share_right("q1")
 
     merge(1)
     merge(2)
-    merge(0)
+    merge(3)
     product(4)
     product(5)
-    product(3)
+    product(6)
     arrived(tan_copies)
     tan = s["tan_r"][...].reshape(128, D).astype(F32)
     for f in range(2):
         tan_ref[f] = jnp.concatenate(
             [tan[16 * t + 8 * f : 16 * t + 8 * f + 8] for t in range(8)], axis=0
         ).astype(BF16)
+    second_stage(0)
     second_stage(1)
     second_stage(2)
-    second_stage(0)
-    merge(4)
-    merge(5)
-    merge(3)
-    third_stage(1)
-    third_stage(2)
-    third_stage(0)
-    second_stage(4)
-    second_stage(5)
     second_stage(3)
-    finish(1)
-    finish(2)
-    finish(0)
-    third_stage(4)
-    third_stage(5)
-    third_stage(3)
-    finish(4)
-    finish(5)
-    finish(3)
+    for job in (5, 6, 4):
+        merge(job)
+    for job in (0, 1, 2, 3):
+        third_stage(job)
+    for job in (5, 6, 4):
+        second_stage(job)
+    for job in (0, 1, 2, 3):
+        finish(job)
+    for job in (5, 6, 4):
+        third_stage(job)
+    for job in (5, 6, 4):
+        finish(job)
 
     for copy in sent:
         copy.wait_send()

time: 69.5 us -> 67.5 us (0.971)
  Pallas kernels: 68.6 us -> 66.7 us
    pallas_call x1, Pallas kernels: 66.7 us -> 64.8 us  [body(): pl.pallas_call(kernel, out_shape=(jax.ShapeDtypeStruct((2, 64, D), BF16),...]
where the time goes in v3:
time: 67.5 us; the launch traced here: 67.3 us
  Pallas kernels  66.7 us (99%)
    pallas_call x1, Pallas kernels, body(): pl.pallas_call(kernel, out_shape=(jax.ShapeDtypeStruct((2, 64, D), BF16),...  64.8 us
    pallas_call x1, Pallas kernels, body(): pl.pallas_call(place, out_shape=(jax.ShapeDtypeStruct((2, 64, D), BF16),...  1.88 us

profile of v3, /device:TPU:1, one launch (start us, length us, event | category | flops | bytes accessed | tf_op | source)
XLA Modules:
  0.0 67.3 jit_solution(8967746694498604686)
XLA Ops:
  0.6 64.8 %shard_map.50 = (bf16[2,64,1152]{2,1,0:T(8,128)(2,1)}, f32[9,4608]{1,0:T(8,128)}) custom-call(bf16[2,64,1152]{2,1,0:T(8,128)(2,1)} %bitcast.2, bf16[1152,4608]{1,0:T(8,128)(2,1)} %params_ref.1, bf16[1152,4608]{1,0:T(8,128)(2,1)} %direction_ref.1), custom_call_target="tpu_custom_call" | custom-call | tf_op jit(solution)/shard_map/pallas_call | solution.py:581
  65.4 1.9 %shard_map.51 = (bf16[2,64,1152]{2,1,0:T(8,128)(2,1)}, f32[9,4608]{1,0:T(8,128)}) custom-call(bf16[2,64,1152]{2,1,0:T(8,128)(2,1)} %get-tuple-element.6.tan_in, f32[9,4608]{1,0:T(8,128)} %get-tuple-element.7.gnv_in), custom_call_target="tpu_custom_call" | custom-call | tf_op jit(solution)/shard_map/pallas_call | solution.py:598

commit v4 on v3

--- a/solution.py
+++ b/solution.py
@@ -22,6 +22,9 @@
     (h * HD, (h + 1) * HD, h * HD // 128 * 128, -(-(h + 1) * HD // 128) * 128)
     for h in range(HEADS)
 ]
+
+ALL = [(0, 1, 2, 3, 4, 5, 6, 7)]
+FIVE_THREE = [(0, 1, 2, 3, 4), (5, 6, 7)]
 
 LEFTS = ["g_z", "g_x", "h2_y", "h2_x", "gy_z", "h1_z", "h1_y", "h1_x"]
 RIGHTS = {"q1": QKV, "o1": OUT, "q2": QKV, "o2": OUT}
@@ -121,44 +124,54 @@
     return left_64(jnp.concatenate(tiles[2:], axis=1))[:, :256].astype(BF16)
 
 
-def attend(qkv, dqkv, kx, dkx, pn_ref, mask, after_head_4):
+def attend(qkv, dqkv, kx, dkx, pn_ref, mask, groups, after_head_4=lambda *_: None):
     out, tan = [None] * 5, [None] * 5
-    for h in range(HEADS):
-        lo, hi, a, b = HEAD_WINDOWS[h]
-        lanes = jnp.where(lane_mask(lo, hi, a, b), 1.0, 0.0).astype(BF16)
-        q = qkv[:, a:b] * lanes
-        both = jnp.concatenate([q, dqkv[:, a:b] * lanes], axis=0)
-        k, dk = kx[:, a:b], dkx[:, a:b]
-        v, dv = qkv[:, 1152 + a : 1152 + b], dqkv[:, 1152 + a : 1152 + b]
-        against_k = nt(both, k)
-        e = jnp.where(mask, jnp.exp(against_k[:128] * SCALE), 0.0)
-        pn = e * (1.0 / jnp.sum(e, axis=1, keepdims=True))
-        pn_ref[h] = pn
-        p = pn.astype(BF16)
-        ds = (against_k[128:] + nt(q, dk)) * SCALE
-        dp = (pn * (ds - jnp.sum(pn * ds, axis=1, keepdims=True))).astype(BF16)
-        against_v = nn(jnp.concatenate([p, dp], axis=0), v)
-        add_head(out, h, against_v[:128])
-        add_head(tan, h, against_v[128:] + nn(p, dv))
-        if h == 4:
-            after_head_4(out, tan)
+    for group in groups:
+        against_k, dk_part, ps = {}, {}, {}
+        for h in group:
+            lo, hi, a, b = HEAD_WINDOWS[h]
+            lanes = jnp.where(lane_mask(lo, hi, a, b), 1.0, 0.0).astype(BF16)
+            q = qkv[:, a:b] * lanes
+            both = jnp.concatenate([q, dqkv[:, a:b] * lanes], axis=0)
+            against_k[h] = nt(both, kx[:, a:b])
+            dk_part[h] = nt(q, dkx[:, a:b])
+        for h in group:
+            e = jnp.where(mask, jnp.exp(against_k[h][:128] * SCALE), 0.0)
+            pn = e * (1.0 / jnp.sum(e, axis=1, keepdims=True))
+            pn_ref[h] = pn
+            ds = (against_k[h][128:] + dk_part[h]) * SCALE
+            dp = pn * (ds - jnp.sum(pn * ds, axis=1, keepdims=True))
+            ps[h] = jnp.concatenate([pn.astype(BF16), dp.astype(BF16)], axis=0)
+        for h in group:
+            lo, hi, a, b = HEAD_WINDOWS[h]
+            against_v = nn(ps[h], qkv[:, 1152 + a : 1152 + b])
+            add_head(out, h, against_v[:128])
+            add_head(tan, h, against_v[128:] + nn(ps[h][:128], dqkv[:, 1152 + a : 1152 + b]))
+            if h == 4:
+                after_head_4(out, tan)
     return out, tan
 
 
-def attend_back(qkv, kx, pn_ref, go, grad_ref, after_head_4):
+def attend_back(qkv, kx, pn_ref, go, grad_ref, groups, after_head_4=lambda: None):
     gq, gk, gv = [None] * 5, [None] * 5, [None] * 5
-    for h in range(HEADS):
-        lo, hi, a, b = HEAD_WINDOWS[h]
-        lanes = jnp.where(lane_mask(lo, hi, a, b), 1.0, 0.0).astype(BF16)
-        gow = go[:, a:b]
-        gp = nt(gow * lanes, qkv[:, 1152 + a : 1152 + b]).astype(BF16).astype(F32)
-        pn = pn_ref[h]
-        gs = (pn * (gp - jnp.sum(gp * pn, axis=1, keepdims=True)) * SCALE).astype(BF16)
-        add_head(gq, h, nn(gs, kx[:, a:b]))
-        add_head(gk, h, tn(gs, qkv[:, a:b]))
-        add_head(gv, h, tn(pn.astype(BF16), gow))
-        if h == 4:
-            after_head_4()
+    for group in groups:
+        gp, gs, gow = {}, {}, {}
+        for h in group:
+            lo, hi, a, b = HEAD_WINDOWS[h]
+            lanes = jnp.where(lane_mask(lo, hi, a, b), 1.0, 0.0).astype(BF16)
+            gow[h] = go[:, a:b]
+            gp[h] = nt(gow[h] * lanes, qkv[:, 1152 + a : 1152 + b])
+        for h in group:
+            pn = pn_ref[h]
+            rounded = gp[h].astype(BF16).astype(F32)
+            gs[h] = (pn * (rounded - jnp.sum(rounded * pn, axis=1, keepdims=True)) * SCALE).astype(BF16)
+        for h in group:
+            lo, hi, a, b = HEAD_WINDOWS[h]
+            add_head(gv, h, tn(pn_ref[h].astype(BF16), gow[h]))
+            add_head(gq, h, nn(gs[h], kx[:, a:b]))
+            add_head(gk, h, tn(gs[h], qkv[:, a:b]))
+            if h == 4:
+                after_head_4()
     gkr = right_64(jnp.concatenate(gk, axis=1))
     for j in range(4):
         grad_ref[:, j * 128 : (j + 1) * 128] = gq[j].astype(BF16)
@@ -230,7 +243,7 @@
     scratch["pad2"] = v((40, 896), F32)
     scratch["ext2"] = v((32, 128), F32)
     scratch["pad3"] = v((16, 512), F32)
-    scratch["w_sem"] = dma((8,))
+    scratch["w_sem"] = dma((10,))
     scratch["a_send"] = dma((5, 7))
     scratch["a_recv"] = dma((5, 7))
     scratch["c_send"] = dma((len(LEFTS) + len(RIGHTS),))
@@ -271,7 +284,8 @@
     sent = []
 
     loads = []
-    for i, (lo, hi) in enumerate([(0, 1792), (1792, 2304), (2304, 4096), (4096, 4608)]):
+    spans = [(0, 1024), (1024, 1792), (1792, 2304), (2304, 4096), (4096, 4608)]
+    for i, (lo, hi) in enumerate(spans):
         pair = []
         for j, (src, dst) in enumerate([(params_ref, s["wp"]), (direction_ref, s["wd"])]):
             copy = pltpu.make_async_copy(src.at[:, lo:hi], dst.at[:, lo:hi], s["w_sem"].at[2 * i + j])
@@ -453,8 +467,9 @@
             gnv_ref[0:8, lanes] = s["pad3"][8 * (j % 2) : 8 * (j % 2) + 8, at : at + 128]
             gnv_ref[8:9, lanes] = s["pad3"][row : row + 1, ninth : ninth + 128]
 
-    loaded(0)
     for lo in range(0, QKV, 256):
+        if lo in (0, 1024):
+            loaded(lo // 1024)
         s["qkv1"][:, lo : lo + 256] = nn(s["h1"][...], s["wp"][:, lo : lo + 256]).astype(BF16)
         s["dqkv1"][:, lo : lo + 256] = nn(s["h1"][...], s["wd"][:, lo : lo + 256]).astype(BF16)
 
@@ -474,7 +489,7 @@
         s["attn_s"][:, :, 384:768] = first_part(tan).reshape(8, 16, 384)
         attn_copies.extend(frame_exchange(1, s["attn_s"], s["attn_r"]))
 
-    o1, do1 = attend(s["qkv1"], s["dqkv1"], s["kx1"], s["dkx"], s["pn1"], same_frame, send_first)
+    o1, do1 = attend(s["qkv1"], s["dqkv1"], s["kx1"], s["dkx"], s["pn1"], same_frame, FIVE_THREE, send_first)
     s["attn2_s"][:, :, 0:256] = second_part(o1).reshape(8, 16, 256)
     s["attn2_s"][:, :, 256:512] = second_part(do1).reshape(8, 16, 256)
     attn_copies.extend(frame_exchange(4, s["attn2_s"], s["attn2_r"]))
@@ -482,23 +497,29 @@
     prepare_left(h1f.astype(BF16).astype(F32), ["h1_z", "h1_y", "h1_x"])
 
     arrived(clips_copies)
-    loaded(1)
-    arrived(attn_copies)
+    loaded(2)
+    s_out, v_sout = s["wp"][:, S_OUT : S_OUT + OUT], s["wd"][:, S_OUT : S_OUT + OUT]
     clips_p = s["clips_r"][...].reshape(128, D).astype(F32)
-    parts = s["attn_r"][...].reshape(128, 768), s["attn2_r"][...].reshape(128, 512)
-    o1x = jnp.concatenate([parts[0][:, :384], parts[1][:, :256]], axis=1)
-    do1x = jnp.concatenate([parts[0][:, 384:], parts[1][:, 256:]], axis=1)
-    s["r_o1"][0:128, :] = o1x
+    arrived(attn_copies[:7])
+    first = s["attn_r"][...].reshape(128, 768)
+    first_both = jnp.concatenate([first[:, :384], first[:, 384:]], axis=0)
+    through = nt(first_both, s_out[:, :384])
+    v_through = nt(first[:, :384], v_sout[:, :384])
+    arrived(attn_copies[7:])
+    second = s["attn2_r"][...].reshape(128, 512)
+    second_both = jnp.concatenate([second[:, :256], second[:, 256:]], axis=0)
+    s["r_o1"][0:128, 0:384] = first[:, :384]
+    s["r_o1"][0:128, 384:640] = second[:, :256]
     share_right("o1")
-    s_out, v_sout = s["wp"][:, S_OUT : S_OUT + OUT], s["wd"][:, S_OUT : S_OUT + OUT]
-    through = nt(jnp.concatenate([o1x, do1x], axis=0), s_out)
+    through = through + nt(second_both, s_out[:, 384:])
+    v_through = v_through + nt(second[:, :256], v_sout[:, 384:])
     y = (clips_p + through[:128]).astype(BF16).astype(F32)
-    dy = (through[128:] + nt(o1x, v_sout)).astype(BF16).astype(F32)
+    dy = (through[128:] + v_through).astype(BF16).astype(F32)
     h2f, rstd = norm_parts(y)
     h2 = h2f.astype(BF16)
     h2_both = jnp.concatenate([h2, norm_tangent(h2f, rstd, dy).astype(BF16)], axis=0)
     prepare_left(h2.astype(F32), ["h2_y", "h2_x"])
-    loaded(2)
+    loaded(3)
     for lo in range(0, QKV, 256):
         wp = s["wp"][:, T_QKV + lo : T_QKV + lo + 256]
         wd = s["wd"][:, T_QKV + lo : T_QKV + lo + 256]
@@ -507,12 +528,12 @@
         s["dqkv2"][:, lo : lo + 256] = (through[128:] + nn(h2, wd)).astype(BF16)
     align_keys(s["qkv2"], s["kx2"])
     align_keys(s["dqkv2"], s["dkx"])
-    o2, do2 = attend(s["qkv2"], s["dqkv2"], s["kx2"], s["dkx"], s["pn2"], same_patch, lambda *_: None)
+    o2, do2 = attend(s["qkv2"], s["dqkv2"], s["kx2"], s["dkx"], s["pn2"], same_patch, ALL)
     o2x = right_64(jnp.concatenate(o2, axis=1)).astype(BF16)
     do2x = right_64(jnp.concatenate(do2, axis=1)).astype(BF16)
     s["r_o2"][0:128, :] = o2x
     share_right("o2")
-    loaded(3)
+    loaded(4)
     t_out, v_tout = s["wp"][:, T_OUT : T_OUT + OUT], s["wd"][:, T_OUT : T_OUT + OUT]
     tangent = (dy + nt(do2x, t_out) + nt(o2x, v_tout)).astype(BF16)
     s["tan_s"][...] = tangent.reshape(8, 16, D)
@@ -520,7 +541,7 @@
     g = (tangent.astype(F32) * (16384 ** (-0.5))).astype(BF16)
     prepare_left(g.astype(F32), ["g_z", "g_x"])
     s["go"][...] = left_64(nn(g, t_out)).astype(BF16)
-    attend_back(s["qkv2"], s["kx2"], s["pn2"], s["go"], s["r_q2"].at[pl.ds(0, 128)], lambda: product(0))
+    attend_back(s["qkv2"], s["kx2"], s["pn2"], s["go"], s["r_q2"].at[pl.ds(0, 128)], FIVE_THREE, lambda: product(0))
     share_right("q2")
     gq2 = s["r_q2"][0:128, :]
     gh2 = nt(gq2, s["wp"][:, T_QKV : T_QKV + QKV])
@@ -536,7 +557,7 @@
 
     arrived(go_copies)
     s["go"][...] = left_64(s["go_r"][...].reshape(128, OUT).astype(F32)).astype(BF16)
-    attend_back(s["qkv1"], s["kx1"], s["pn1"], s["go"], s["r_q1"].at[pl.ds(0, 128)], lambda: None)
+    attend_back(s["qkv1"], s["kx1"], s["pn1"], s["go"], s["r_q1"].at[pl.ds(0, 128)], ALL)
     share_right("q1")
 
     merge(1)

time: 67.5 us -> 65 us (0.963)
  Pallas kernels: 66.7 us -> 63.5 us
    pallas_call x1, Pallas kernels: 64.8 us -> 61.6 us  [body(): pl.pallas_call(kernel, out_shape=(jax.ShapeDtypeStruct((2, 64, D), BF16),...]
where the time goes in v4:
time: 65 us; the launch traced here: 64.2 us
  Pallas kernels  63.5 us (98%)
    pallas_call x1, Pallas kernels, body(): pl.pallas_call(kernel, out_shape=(jax.ShapeDtypeStruct((2, 64, D), BF16),...  61.6 us
    pallas_call x1, Pallas kernels, body(): pl.pallas_call(place, out_shape=(jax.ShapeDtypeStruct((2, 64, D), BF16),...  1.88 us

profile of v4, /device:TPU:1, one launch (start us, length us, event | category | flops | bytes accessed | tf_op | source)
XLA Modules:
  0.0 64.2 jit_solution(9163306398328386579)
XLA Ops:
  0.6 61.6 %shard_map.50 = (bf16[2,64,1152]{2,1,0:T(8,128)(2,1)}, f32[9,4608]{1,0:T(8,128)}) custom-call(bf16[2,64,1152]{2,1,0:T(8,128)(2,1)} %bitcast.2, bf16[1152,4608]{1,0:T(8,128)(2,1)} %params_ref.1, bf16[1152,4608]{1,0:T(8,128)(2,1)} %direction_ref.1), custom_call_target="tpu_custom_call" | custom-call | tf_op jit(solution)/shard_map/pallas_call | solution.py:602
  62.3 1.9 %shard_map.51 = (bf16[2,64,1152]{2,1,0:T(8,128)(2,1)}, f32[9,4608]{1,0:T(8,128)}) custom-call(bf16[2,64,1152]{2,1,0:T(8,128)(2,1)} %get-tuple-element.6.tan_in, f32[9,4608]{1,0:T(8,128)} %get-tuple-element.7.gnv_in), custom_call_target="tpu_custom_call" | custom-call | tf_op jit(solution)/shard_map/pallas_call | solution.py:619

commit v5 on v4

--- a/solution.py
+++ b/solution.py
@@ -1,3 +1,5 @@
+from types import SimpleNamespace
+
 import jax
 import jax.numpy as jnp
 from jax import lax
@@ -49,6 +51,7 @@
     (0, 640, "xyz", [(0, 640, [("h1_x", "q1", 0)])]),
 ]
 N_JOBS = len(JOBS)
+AT_ONCE = (4, 5, 6)
 
 
 def third_width(n):
@@ -230,14 +233,14 @@
     for name, width in RIGHTS.items():
         scratch["r_" + name] = v((256, width), BF16)
     for i, (_, n, _, _) in enumerate(JOBS):
-        scratch[f"p{i}"] = v((4, 144, n), BF16)
-        scratch[f"u{i}"] = v((144, n), BF16)
-        scratch[f"m{i}"] = v((144, n), BF16)
-        scratch[f"v{i}"] = v((2, 144, n), BF16)
-        scratch[f"s2_{i}"] = v((4, 32, n + 128), BF16)
-        scratch[f"v2_{i}"] = v((3, 32, n + 128), BF16)
-        scratch[f"s3_{i}"] = v((4, 16, third_width(n)), BF16)
-        scratch[f"v3_{i}"] = v((3, 16, third_width(n)), BF16)
+        scratch["p_%d" % i] = v((4, 144, n), BF16)
+        scratch["u_%d" % i] = v((144, n), BF16)
+        scratch["m_%d" % i] = v((144, n), BF16)
+        scratch["v_%d" % i] = v((3 if i in AT_ONCE else 2, 144, n), BF16)
+        scratch["s2_%d" % i] = v((4, 32, n + 128), BF16)
+        scratch["v2_%d" % i] = v((3, 32, n + 128), BF16)
+        scratch["s3_%d" % i] = v((4, 16, third_width(n)), BF16)
+        scratch["v3_%d" % i] = v((3, 16, third_width(n)), BF16)
     scratch["acc1"] = v((144, 896), F32)
     scratch["acc2"] = v((40, 896), F32)
     scratch["pad2"] = v((40, 896), F32)
@@ -257,7 +260,11 @@
 
 
 def kernel(clips_ref, params_ref, direction_ref, tan_ref, gnv_ref, *scratch_refs):
-    s = dict(zip(SCRATCH, scratch_refs))
+    refs = dict(zip(SCRATCH, scratch_refs))
+    s = SimpleNamespace(**refs)
+    for key in ("p", "u", "m", "v", "s2", "v2", "s3", "v3"):
+        setattr(s, key, [refs[key + "_%d" % i] for i in range(N_JOBS)])
+    s.rights = {name: refs["r_" + name] for name in RIGHTS}
     dp, fr = lax.axis_index("dp"), lax.axis_index("frame")
     core, y_hi, z = dp % 2, dp // 2 % 2, dp // 4
     x, y_lo = fr // 2, fr % 2
@@ -287,8 +294,8 @@
     spans = [(0, 1024), (1024, 1792), (1792, 2304), (2304, 4096), (4096, 4608)]
     for i, (lo, hi) in enumerate(spans):
         pair = []
-        for j, (src, dst) in enumerate([(params_ref, s["wp"]), (direction_ref, s["wd"])]):
-            copy = pltpu.make_async_copy(src.at[:, lo:hi], dst.at[:, lo:hi], s["w_sem"].at[2 * i + j])
+        for j, (src, dst) in enumerate([(params_ref, s.wp), (direction_ref, s.wd)]):
+            copy = pltpu.make_async_copy(src.at[:, lo:hi], dst.at[:, lo:hi], s.w_sem.at[2 * i + j])
             copy.start()
             pair.append(copy)
         loads.append(pair)
@@ -308,9 +315,9 @@
     tokens = jnp.concatenate(
         [natural[f, 8 * t : 8 * t + 8] for t in range(8) for f in range(2)], axis=0
     )
-    s["clips_s"][...] = tokens.astype(BF16).reshape(8, 16, D)
+    s.clips_s[...] = tokens.astype(BF16).reshape(8, 16, D)
     h1f, _ = norm_parts(tokens)
-    s["h1"][...] = h1f.astype(BF16)
+    s.h1[...] = h1f.astype(BF16)
 
     pl.semaphore_wait(barrier, len(peers))
 
@@ -319,7 +326,7 @@
         for k in range(1, 8):
             t = (fr + k) % 8
             copies.append(
-                remote(src.at[t], dst.at[fr], s["a_send"].at[which, k - 1], s["a_recv"].at[which, k - 1], (dp, t))
+                remote(src.at[t], dst.at[fr], s.a_send.at[which, k - 1], s.a_recv.at[which, k - 1], (dp, t))
             )
         dst[fr] = src[fr]
         return copies
@@ -328,33 +335,33 @@
         for copy in copies:
             copy.wait_recv()
 
-    clips_copies = frame_exchange(0, s["clips_s"], s["clips_r"])
+    clips_copies = frame_exchange(0, s.clips_s, s.clips_r)
 
     left_copies = {}
 
     def prepare_left(value, names):
-        s["lt"][...] = value.T
+        s.lt[...] = value.T
         for name in names:
             i = LEFTS.index(name)
             for src, c, dst, rows in row_moves(name[-1]):
-                s["lts"][c, dst : dst + rows, :] = s["lt"][src : src + rows, :]
-            s["left"][i, :, 0:128] = s["lts"][core].astype(BF16)
-            s["left_s"][i] = s["lts"][1 - core].astype(BF16)
+                s.lts[c, dst : dst + rows, :] = s.lt[src : src + rows, :]
+            s.left[i, :, 0:128] = s.lts[core].astype(BF16)
+            s.left_s[i] = s.lts[1 - core].astype(BF16)
             left_copies[name] = remote(
-                s["left_s"].at[i], s["left"].at[i, :, pl.ds(128, 128)], s["c_send"].at[i], s["c_recv"].at[i], partner
+                s.left_s.at[i], s.left.at[i, :, pl.ds(128, 128)], s.c_send.at[i], s.c_recv.at[i], partner
             )
 
     right_copies = {}
 
     def share_right(name):
         i = len(LEFTS) + list(RIGHTS).index(name)
-        ref = s["r_" + name]
+        ref = s.rights[name]
         right_copies[name] = remote(
-            ref.at[pl.ds(0, 128)], ref.at[pl.ds(128, 128)], s["c_send"].at[i], s["c_recv"].at[i], partner
+            ref.at[pl.ds(0, 128)], ref.at[pl.ds(128, 128)], s.c_send.at[i], s.c_recv.at[i], partner
         )
 
-    s["ext2"][...] = jnp.zeros_like(s["ext2"])
-    s["pad3"][...] = jnp.zeros_like(s["pad3"])
+    s.ext2[...] = jnp.zeros_like(s.ext2)
+    s.pad3[...] = jnp.zeros_like(s.pad3)
     flight = {}
     shared = []
 
@@ -366,18 +373,30 @@
             if name not in shared:
                 copies[name].wait_recv()
                 shared.append(name)
-        part, first_in, ready = s[f"p{job}"], s[f"u{job}"], s[f"v{job}"]
+        part, first_in, ready = s.p[job], s.u[job], s.v[job]
         for lo, hi, terms in segments:
             acc = None
             for left, right, at in terms:
-                term = nn(s["left"][LEFTS.index(left)], s["r_" + right][:, at : at + hi - lo])
+                term = nn(s.left[LEFTS.index(left)], s.rights[right][:, at : at + hi - lo])
                 acc = term if acc is None else acc + term
             part[:, :, lo:hi] = acc.astype(BF16).reshape(4, 144, hi - lo)
         here = where[axes[0]]
+        if job in AT_ONCE:
+            flight[job] = [
+                remote(
+                    part.at[(here + k) % 4],
+                    ready.at[k - 1],
+                    s.rs_send.at[job, k - 1],
+                    s.rs_recv.at[job, k - 1],
+                    along(axes[0], k),
+                )
+                for k in (2, 1, 3)
+            ]
+            return
         right, left = along(axes[0], 1), along(axes[0], 3)
         ahead, behind, across = (here + 1) % 4, (here + 3) % 4, (here + 2) % 4
         flight[job] = [
-            remote(src.at[pl.ds(at, rows)], dst.at[pl.ds(at, rows)], s["rs_send"].at[job, i], s["rs_recv"].at[job, i], to)
+            remote(src.at[pl.ds(at, rows)], dst.at[pl.ds(at, rows)], s.rs_send.at[job, i], s.rs_recv.at[job, i], to)
             for i, (src, dst, at, rows, to) in enumerate(
                 [
                     (part.at[across], first_in, 0, 80, right),
@@ -389,8 +408,10 @@
         ]
 
     def merge(job):
+        if job in AT_ONCE:
+            return
         here = where[JOBS[job][2][0]]
-        part, first_in, merged, ready = s[f"p{job}"], s[f"u{job}"], s[f"m{job}"], s[f"v{job}"]
+        part, first_in, merged, ready = s.p[job], s.u[job], s.m[job], s.v[job]
         for i, k, at, rows in [(0, 1, 0, 80), (1, 3, 80, 64)]:
             flight[job][i].wait_recv()
             own = part[(here + k) % 4, at : at + rows].astype(F32)
@@ -399,8 +420,8 @@
                 remote(
                     merged.at[pl.ds(at, rows)],
                     ready.at[i, pl.ds(at, rows)],
-                    s["rs_send"].at[job, 4 + i],
-                    s["rs_recv"].at[job, 4 + i],
+                    s.rs_send.at[job, 4 + i],
+                    s.rs_recv.at[job, 4 + i],
                     along(JOBS[job][2][0], k),
                 )
             )
@@ -414,26 +435,27 @@
                 remote(
                     src.at[(where[axis] + k) % 4],
                     dst.at[k - 1],
-                    s["rs_send"].at[job, i],
-                    s["rs_recv"].at[job, i],
+                    s.rs_send.at[job, i],
+                    s.rs_recv.at[job, i],
                     along(axis, k),
                 )
             )
 
     def second_stage(job):
         _, n, axes, _ = JOBS[job]
-        arrived(flight[job][2:])
-        part, ready = s[f"p{job}"], s[f"v{job}"]
-        s["acc1"][:, :n] = part[where[axes[0]]].astype(F32) + ready[0].astype(F32) + ready[1].astype(F32)
+        arrived(flight[job] if job in AT_ONCE else flight[job][2:])
+        part, ready = s.p[job], s.v[job]
+        acc = part[where[axes[0]]].astype(F32) + ready[0].astype(F32) + ready[1].astype(F32)
+        s.acc1[:, :n] = acc + ready[2].astype(F32) if job in AT_ONCE else acc
         for second in range(4):
             for third in range(4):
                 at = second_rows(axes, second, third)
-                s["pad2"][9 * third : 9 * third + 9, :n] = s["acc1"][at : at + 9, :n]
+                s.pad2[9 * third : 9 * third + 9, :n] = s.acc1[at : at + 9, :n]
             for j in range(n // 128):
-                s["ext2"][4 * j : 4 * j + 4] = s["pad2"][32:36, 128 * j : 128 * j + 128]
-            s[f"s2_{job}"][second, :, :n] = s["pad2"][0:32, :n].astype(BF16)
-            s[f"s2_{job}"][second, :, n:] = s["ext2"][...].astype(BF16)
-        scatter(job, 1, s[f"s2_{job}"], s[f"v2_{job}"])
+                s.ext2[4 * j : 4 * j + 4] = s.pad2[32:36, 128 * j : 128 * j + 128]
+            s.s2[job][second, :, :n] = s.pad2[0:32, :n].astype(BF16)
+            s.s2[job][second, :, n:] = s.ext2[...].astype(BF16)
+        scatter(job, 1, s.s2[job], s.v2[job])
 
     def total(job, stage, src, dst):
         arrived(flight[job])
@@ -443,35 +465,35 @@
     def third_stage(job):
         n = JOBS[job][1]
         tiles, width = n // 128, third_width(n)
-        sums = total(job, 1, s[f"s2_{job}"], s[f"v2_{job}"])
-        s["acc2"][0:32, :n] = sums[:, :n]
-        s["ext2"][...] = sums[:, n:]
+        sums = total(job, 1, s.s2[job], s.v2[job])
+        s.acc2[0:32, :n] = sums[:, :n]
+        s.ext2[...] = sums[:, n:]
         for j in range(tiles):
-            s["acc2"][32:36, 128 * j : 128 * j + 128] = s["ext2"][4 * j : 4 * j + 4]
+            s.acc2[32:36, 128 * j : 128 * j + 128] = s.ext2[4 * j : 4 * j + 4]
         for third in range(4):
             for j in range(tiles):
                 lanes, at, ninth = slice(128 * j, 128 * j + 128), 128 * (j // 2), 128 * (tiles // 2)
-                s["pad3"][8 * (j % 2) : 8 * (j % 2) + 8, at : at + 128] = s["acc2"][9 * third : 9 * third + 8, lanes]
+                s.pad3[8 * (j % 2) : 8 * (j % 2) + 8, at : at + 128] = s.acc2[9 * third : 9 * third + 8, lanes]
                 row = 8 * (tiles % 2) + j
-                s["pad3"][row : row + 1, ninth : ninth + 128] = s["acc2"][9 * third + 8 : 9 * third + 9, lanes]
-            s[f"s3_{job}"][third] = s["pad3"][:, :width].astype(BF16)
-        scatter(job, 2, s[f"s3_{job}"], s[f"v3_{job}"])
+                s.pad3[row : row + 1, ninth : ninth + 128] = s.acc2[9 * third + 8 : 9 * third + 9, lanes]
+            s.s3[job][third] = s.pad3[:, :width].astype(BF16)
+        scatter(job, 2, s.s3[job], s.v3[job])
 
     def finish(job):
         first, n, _, _ = JOBS[job]
         tiles, width = n // 128, third_width(n)
-        s["pad3"][:, :width] = total(job, 2, s[f"s3_{job}"], s[f"v3_{job}"])
+        s.pad3[:, :width] = total(job, 2, s.s3[job], s.v3[job])
         for j in range(tiles):
             lanes, at, ninth = slice(first + 128 * j, first + 128 * j + 128), 128 * (j // 2), 128 * (tiles // 2)
             row = 8 * (tiles % 2) + j
-            gnv_ref[0:8, lanes] = s["pad3"][8 * (j % 2) : 8 * (j % 2) + 8, at : at + 128]
-            gnv_ref[8:9, lanes] = s["pad3"][row : row + 1, ninth : ninth + 128]
+            gnv_ref[0:8, lanes] = s.pad3[8 * (j % 2) : 8 * (j % 2) + 8, at : at + 128]
+            gnv_ref[8:9, lanes] = s.pad3[row : row + 1, ninth : ninth + 128]
 
     for lo in range(0, QKV, 256):
         if lo in (0, 1024):
             loaded(lo // 1024)
-        s["qkv1"][:, lo : lo + 256] = nn(s["h1"][...], s["wp"][:, lo : lo + 256]).astype(BF16)
-        s["dqkv1"][:, lo : lo + 256] = nn(s["h1"][...], s["wd"][:, lo : lo + 256]).astype(BF16)
+        s.qkv1[:, lo : lo + 256] = nn(s.h1[...], s.wp[:, lo : lo + 256]).astype(BF16)
+        s.dqkv1[:, lo : lo + 256] = nn(s.h1[...], s.wd[:, lo : lo + 256]).astype(BF16)
 
     def align_keys(qkv, kx):
         kx[...] = left_64(qkv[:, 512:1152].astype(F32)).astype(BF16)
@@ -480,36 +502,36 @@
     col = lax.broadcasted_iota(jnp.int32, (128, 128), 1)
     same_frame = row // 8 % 2 == col // 8 % 2
     same_patch = row % 8 == col % 8
-    align_keys(s["qkv1"], s["kx1"])
-    align_keys(s["dqkv1"], s["dkx"])
+    align_keys(s.qkv1, s.kx1)
+    align_keys(s.dqkv1, s.dkx)
     attn_copies = []
 
     def send_first(out, tan):
-        s["attn_s"][:, :, 0:384] = first_part(out).reshape(8, 16, 384)
-        s["attn_s"][:, :, 384:768] = first_part(tan).reshape(8, 16, 384)
-        attn_copies.extend(frame_exchange(1, s["attn_s"], s["attn_r"]))
-
-    o1, do1 = attend(s["qkv1"], s["dqkv1"], s["kx1"], s["dkx"], s["pn1"], same_frame, FIVE_THREE, send_first)
-    s["attn2_s"][:, :, 0:256] = second_part(o1).reshape(8, 16, 256)
-    s["attn2_s"][:, :, 256:512] = second_part(do1).reshape(8, 16, 256)
-    attn_copies.extend(frame_exchange(4, s["attn2_s"], s["attn2_r"]))
+        s.attn_s[:, :, 0:384] = first_part(out).reshape(8, 16, 384)
+        s.attn_s[:, :, 384:768] = first_part(tan).reshape(8, 16, 384)
+        attn_copies.extend(frame_exchange(1, s.attn_s, s.attn_r))
+
+    o1, do1 = attend(s.qkv1, s.dqkv1, s.kx1, s.dkx, s.pn1, same_frame, FIVE_THREE, send_first)
+    s.attn2_s[:, :, 0:256] = second_part(o1).reshape(8, 16, 256)
+    s.attn2_s[:, :, 256:512] = second_part(do1).reshape(8, 16, 256)
+    attn_copies.extend(frame_exchange(4, s.attn2_s, s.attn2_r))
 
     prepare_left(h1f.astype(BF16).astype(F32), ["h1_z", "h1_y", "h1_x"])
 
     arrived(clips_copies)
     loaded(2)
-    s_out, v_sout = s["wp"][:, S_OUT : S_OUT + OUT], s["wd"][:, S_OUT : S_OUT + OUT]
-    clips_p = s["clips_r"][...].reshape(128, D).astype(F32)
+    s_out, v_sout = s.wp[:, S_OUT : S_OUT + OUT], s.wd[:, S_OUT : S_OUT + OUT]
+    clips_p = s.clips_r[...].reshape(128, D).astype(F32)
     arrived(attn_copies[:7])
-    first = s["attn_r"][...].reshape(128, 768)
+    first = s.attn_r[...].reshape(128, 768)
     first_both = jnp.concatenate([first[:, :384], first[:, 384:]], axis=0)
     through = nt(first_both, s_out[:, :384])
     v_through = nt(first[:, :384], v_sout[:, :384])
     arrived(attn_copies[7:])
-    second = s["attn2_r"][...].reshape(128, 512)
+    second = s.attn2_r[...].reshape(128, 512)
     second_both = jnp.concatenate([second[:, :256], second[:, 256:]], axis=0)
-    s["r_o1"][0:128, 0:384] = first[:, :384]
-    s["r_o1"][0:128, 384:640] = second[:, :256]
+    s.r_o1[0:128, 0:384] = first[:, :384]
+    s.r_o1[0:128, 384:640] = second[:, :256]
     share_right("o1")
     through = through + nt(second_both, s_out[:, 384:])
     v_through = v_through + nt(second[:, :256], v_sout[:, 384:])
@@ -521,33 +543,33 @@
     prepare_left(h2.astype(F32), ["h2_y", "h2_x"])
     loaded(3)
     for lo in range(0, QKV, 256):
-        wp = s["wp"][:, T_QKV + lo : T_QKV + lo + 256]
-        wd = s["wd"][:, T_QKV + lo : T_QKV + lo + 256]
+        wp = s.wp[:, T_QKV + lo : T_QKV + lo + 256]
+        wd = s.wd[:, T_QKV + lo : T_QKV + lo + 256]
         through = nn(h2_both, wp)
-        s["qkv2"][:, lo : lo + 256] = through[:128].astype(BF16)
-        s["dqkv2"][:, lo : lo + 256] = (through[128:] + nn(h2, wd)).astype(BF16)
-    align_keys(s["qkv2"], s["kx2"])
-    align_keys(s["dqkv2"], s["dkx"])
-    o2, do2 = attend(s["qkv2"], s["dqkv2"], s["kx2"], s["dkx"], s["pn2"], same_patch, ALL)
+        s.qkv2[:, lo : lo + 256] = through[:128].astype(BF16)
+        s.dqkv2[:, lo : lo + 256] = (through[128:] + nn(h2, wd)).astype(BF16)
+    align_keys(s.qkv2, s.kx2)
+    align_keys(s.dqkv2, s.dkx)
+    o2, do2 = attend(s.qkv2, s.dqkv2, s.kx2, s.dkx, s.pn2, same_patch, ALL)
     o2x = right_64(jnp.concatenate(o2, axis=1)).astype(BF16)
     do2x = right_64(jnp.concatenate(do2, axis=1)).astype(BF16)
-    s["r_o2"][0:128, :] = o2x
+    s.r_o2[0:128, :] = o2x
     share_right("o2")
     loaded(4)
-    t_out, v_tout = s["wp"][:, T_OUT : T_OUT + OUT], s["wd"][:, T_OUT : T_OUT + OUT]
+    t_out, v_tout = s.wp[:, T_OUT : T_OUT + OUT], s.wd[:, T_OUT : T_OUT + OUT]
     tangent = (dy + nt(do2x, t_out) + nt(o2x, v_tout)).astype(BF16)
-    s["tan_s"][...] = tangent.reshape(8, 16, D)
-    tan_copies = frame_exchange(3, s["tan_s"], s["tan_r"])
+    s.tan_s[...] = tangent.reshape(8, 16, D)
+    tan_copies = frame_exchange(3, s.tan_s, s.tan_r)
     g = (tangent.astype(F32) * (16384 ** (-0.5))).astype(BF16)
     prepare_left(g.astype(F32), ["g_z", "g_x"])
-    s["go"][...] = left_64(nn(g, t_out)).astype(BF16)
-    attend_back(s["qkv2"], s["kx2"], s["pn2"], s["go"], s["r_q2"].at[pl.ds(0, 128)], FIVE_THREE, lambda: product(0))
+    s.go[...] = left_64(nn(g, t_out)).astype(BF16)
+    attend_back(s.qkv2, s.kx2, s.pn2, s.go, s.r_q2.at[pl.ds(0, 128)], FIVE_THREE, lambda: product(0))
     share_right("q2")
-    gq2 = s["r_q2"][0:128, :]
-    gh2 = nt(gq2, s["wp"][:, T_QKV : T_QKV + QKV])
+    gq2 = s.r_q2[0:128, :]
+    gh2 = nt(gq2, s.wp[:, T_QKV : T_QKV + QKV])
     gy = (g.astype(F32) + norm_tangent(h2f, rstd, gh2)).astype(BF16)
-    s["go_s"][...] = nn(gy, s_out).astype(BF16).reshape(8, 16, OUT)
-    go_copies = frame_exchange(2, s["go_s"], s["go_r"])
+    s.go_s[...] = nn(gy, s_out).astype(BF16).reshape(8, 16, OUT)
+    go_copies = frame_exchange(2, s.go_s, s.go_r)
 
     prepare_left(gy.astype(F32), ["gy_z"])
     product(1)
@@ -556,8 +578,8 @@
     merge(0)
 
     arrived(go_copies)
-    s["go"][...] = left_64(s["go_r"][...].reshape(128, OUT).astype(F32)).astype(BF16)
-    attend_back(s["qkv1"], s["kx1"], s["pn1"], s["go"], s["r_q1"].at[pl.ds(0, 128)], ALL)
+    s.go[...] = left_64(s.go_r[...].reshape(128, OUT).astype(F32)).astype(BF16)
+    attend_back(s.qkv1, s.kx1, s.pn1, s.go, s.r_q1.at[pl.ds(0, 128)], ALL)
     share_right("q1")
 
     merge(1)
@@ -566,26 +588,26 @@
     product(4)
     product(5)
     product(6)
-    arrived(tan_copies)
-    tan = s["tan_r"][...].reshape(128, D).astype(F32)
-    for f in range(2):
-        tan_ref[f] = jnp.concatenate(
-            [tan[16 * t + 8 * f : 16 * t + 8 * f + 8] for t in range(8)], axis=0
-        ).astype(BF16)
     second_stage(0)
     second_stage(1)
     second_stage(2)
     second_stage(3)
     for job in (5, 6, 4):
         merge(job)
+    for job in (5, 6, 4):
+        second_stage(job)
     for job in (0, 1, 2, 3):
         third_stage(job)
     for job in (5, 6, 4):
-        second_stage(job)
+        third_stage(job)
+    arrived(tan_copies)
+    tan = s.tan_r[...].reshape(128, D).astype(F32)
+    for f in range(2):
+        tan_ref[f] = jnp.concatenate(
+            [tan[16 * t + 8 * f : 16 * t + 8 * f + 8] for t in range(8)], axis=0
+        ).astype(BF16)
     for job in (0, 1, 2, 3):
         finish(job)
-    for job in (5, 6, 4):
-        third_stage(job)
     for job in (5, 6, 4):
         finish(job)
 

time: 65 us -> 63.8 us (0.982)
  Pallas kernels: 63.5 us -> 62.5 us
    pallas_call x1, Pallas kernels: 61.6 us -> 60.6 us  [body(): pl.pallas_call(kernel, out_shape=(jax.ShapeDtypeStruct((2, 64, D), BF16),...]
where the time goes in v5:
time: 63.8 us; the launch traced here: 63.1 us
  Pallas kernels  62.5 us (98%)
  between operations  0.64 us (1%)
    pallas_call x1, Pallas kernels, body(): pl.pallas_call(kernel, out_shape=(jax.ShapeDtypeStruct((2, 64, D), BF16),...  60.6 us
    pallas_call x1, Pallas kernels, body(): pl.pallas_call(place, out_shape=(jax.ShapeDtypeStruct((2, 64, D), BF16),...  1.88 us

profile of v5, /device:TPU:1, one launch (start us, length us, event | category | flops | bytes accessed | tf_op | source)
XLA Modules:
  0.0 63.1 jit_solution(3893055623455737306)
XLA Ops:
  0.6 60.6 %shard_map.50 = (bf16[2,64,1152]{2,1,0:T(8,128)(2,1)}, f32[9,4608]{1,0:T(8,128)}) custom-call(bf16[2,64,1152]{2,1,0:T(8,128)(2,1)} %bitcast.2, bf16[1152,4608]{1,0:T(8,128)(2,1)} %params_ref.1, bf16[1152,4608]{1,0:T(8,128)(2,1)} %direction_ref.1), custom_call_target="tpu_custom_call" | custom-call | tf_op jit(solution)/shard_map/pallas_call | solution.py:624
  61.2 1.9 %shard_map.51 = (bf16[2,64,1152]{2,1,0:T(8,128)(2,1)}, f32[9,4608]{1,0:T(8,128)}) custom-call(bf16[2,64,1152]{2,1,0:T(8,128)(2,1)} %get-tuple-element.6.tan_in, f32[9,4608]{1,0:T(8,128)} %get-tuple-element.7.gnv_in), custom_call_target="tpu_custom_call" | custom-call | tf_op jit(solution)/shard_map/pallas_call | solution.py:641
